TPU v7x, 512 devices: a whole 4x8x8 slice. The times are simulated.
512 devices in a mesh: pipe: 64 (over y, z_hi, core), tensor: 8 (over z_lo, x).
Axes of the slice: x: 4, y: 8, z: 8 (z_hi: 4, z_lo: 2; z = z_hi * 2 + z_lo), core: 2. Of those that a mesh axis runs over, the one named last changes fastest.
Arguments:
- queries: bfloat16 [64, 128, 4096], P('pipe', None, 'tensor'), may hold values from -6 to 6
- keys: bfloat16 [64, 128, 1024], P('pipe', None, 'tensor'), may hold values from -6 to 6
- values: bfloat16 [64, 128, 1024], P('pipe', None, 'tensor'), may hold values from -6 to 6
- out_grad: bfloat16 [64, 128, 4096], P('pipe', None, 'tensor'), may hold values from -18 to 18
- key_weight: bfloat16 [64, 4096, 1024], P('pipe', None, 'tensor'), may hold values from -0.09375 to 0.09375
- value_weight: bfloat16 [64, 4096, 1024], P('pipe', None, 'tensor'), may hold values from -0.09375 to 0.09375
- head_gate: float32 [64, 32], P('pipe', 'tensor'), may hold values from 0.4 to 1.2
- layer_gate: float32 [64], P('pipe'), may hold values from 0.5 to 1.5
- head_order: int32 [64, 32], P('pipe'), may hold values from 0 to 31, each once within a row
Outputs:
- input_grad: bfloat16 [64, 128, 4096], P('pipe', None, 'tensor')
- head_grad: float32 [64, 32], P('pipe', 'tensor')
- layer_grad: float32 [64], P('pipe')
Inputs may be any that keep to these rules, and one draw needn't show every extreme that they name: `head_order`: the first 8 entries of each layer's row name its masked heads.
All inputs are finite; a program needn't handle non-finite values.
Results may differ from a plain program's by a relative error of at most 0.019.
Values may be sent and summed in bfloat16 or wider, within the bound.
No kernel may reach another device: no remote copies, remote signals or barrier semaphores. Data moves between devices by JAX's collectives and lax.ppermute only.
A program may use at most 64 MiB of HBM per device.

v0:
```python
import jax
import jax.numpy as jnp
from jax import lax
from jax.sharding import PartitionSpec as P

HEAD = 128
MASKED = 8


def prefix(x, axis, combine, identity):
    size, place = (lax.axis_size(axis), lax.axis_index(axis))
    everything = lax.all_gather(x.astype(jnp.bfloat16), axis)
    start = jnp.broadcast_to(jnp.asarray(identity, x.dtype), x.shape)

    def turn(k, before):
        at = size - 1 - k
        reached = at > place
        new = combine(before, everything[at].astype(x.dtype))
        return jnp.where(reached, new, before)

    return lax.fori_loop(0, size, turn, start)


def add_terms(earlier, later_part):
    return earlier + later_part


def body(
    queries, keys, values, out_grad, key_weight, value_weight, head_gate, layer_gate, head_order
):
    seq_len = queries.shape[1]
    heads_here = head_gate.shape[1]
    kv_here = keys.shape[2] // HEAD
    group_size = heads_here // kv_here
    tensor_size = lax.axis_size("tensor")
    shard_width = key_weight.shape[1] // tensor_size
    tensor_place = lax.axis_index("tensor")
    score_scale = HEAD ** (-0.5)
    query_heads = queries[0].reshape(seq_len, kv_here, group_size, HEAD)
    key_heads = keys[0].reshape(seq_len, kv_here, HEAD)
    value_heads = values[0].reshape(seq_len, kv_here, HEAD)
    grad_heads = out_grad[0].reshape(seq_len, kv_here, group_size, HEAD)
    scores = (
        jnp.einsum("skgd,tkd->kgst", query_heads, key_heads, preferred_element_type=jnp.float32)
        * score_scale
    )
    row_index = lax.broadcasted_iota(jnp.int32, (seq_len, seq_len), 0)
    col_index = lax.broadcasted_iota(jnp.int32, (seq_len, seq_len), 1)
    scores = jnp.where(row_index >= col_index, scores, -1e30)
    row_max = jnp.max(scores, axis=-1, keepdims=True)
    expo = jnp.exp(scores - row_max)
    attention = expo / jnp.sum(expo, axis=-1, keepdims=True)
    probs_half = attention.astype(jnp.bfloat16)
    attended = jnp.einsum(
        "kgst,tkd->skgd", probs_half, value_heads, preferred_element_type=jnp.float32
    )
    head_sums = jnp.sum(grad_heads.astype(jnp.float32) * attended, axis=(0, 3)).reshape(heads_here)
    listed = head_order[0, :MASKED]
    head_ids = tensor_place * heads_here + jnp.arange(heads_here, dtype=jnp.int32)
    masked = jnp.any(listed[:, None] == head_ids[None, :], axis=0)
    open_gate = head_gate[0] * jnp.where(masked, 0.0, 1.0)
    layer_value = layer_gate[0]
    gate_values = (layer_value * open_gate).reshape(kv_here, group_size)
    scaled_grad = (grad_heads.astype(jnp.float32) * gate_values[None, :, :, None]).astype(
        jnp.bfloat16
    )
    prob_grad = jnp.einsum(
        "skgd,tkd->kgst", scaled_grad, value_heads, preferred_element_type=jnp.float32
    )
    centre = jnp.sum(attention * prob_grad, axis=-1, keepdims=True)
    score_grad = (attention * (prob_grad - centre) * score_scale).astype(jnp.bfloat16)
    key_grad = jnp.einsum(
        "kgst,skgd->tkd", score_grad, query_heads, preferred_element_type=jnp.float32
    )
    key_grad = key_grad.astype(jnp.bfloat16).reshape(seq_len, kv_here * HEAD)
    value_grad = jnp.einsum(
        "kgst,skgd->tkd", probs_half, scaled_grad, preferred_element_type=jnp.float32
    )
    value_grad = value_grad.astype(jnp.bfloat16).reshape(seq_len, kv_here * HEAD)
    key_rows = key_weight[0]
    value_rows = value_weight[0]
    contract = (((1,), (1,)), ((), ()))
    partial_value = lax.dot_general(
        key_grad, key_rows, contract, preferred_element_type=jnp.float32
    )
    partial_value = partial_value + lax.dot_general(
        value_grad, value_rows, contract, preferred_element_type=jnp.float32
    )
    summed = lax.psum(partial_value.astype(jnp.bfloat16), "tensor").astype(jnp.float32)
    section_term = lax.dynamic_slice_in_dim(summed, tensor_place * shard_width, shard_width, 1)
    above_sum = prefix(section_term, "pipe", add_terms, jnp.zeros_like(section_term))
    input_grad = (section_term + above_sum).astype(jnp.bfloat16)[None]
    head_grad = (layer_value * head_sums)[None]
    products = lax.all_gather(open_gate * head_sums, "tensor", axis=0, tiled=True)
    layer_grad = jnp.sum(products)[None]
    return (input_grad, head_grad, layer_grad)


def solution(mesh):
    placed = (
        P("pipe", None, "tensor"),
        P("pipe", None, "tensor"),
        P("pipe", None, "tensor"),
        P("pipe", None, "tensor"),
        P("pipe", None, "tensor"),
        P("pipe", None, "tensor"),
        P("pipe", "tensor"),
        P("pipe"),
        P("pipe", None),
    )
    return jax.shard_map(
        body,
        mesh=mesh,
        in_specs=placed,
        out_specs=(P("pipe", None, "tensor"), P("pipe", "tensor"), P("pipe")),
        check_vma=False,
    )
```

profile of v0, /device:TPU:1, one launch (start us, length us, event | category | flops | bytes accessed | tf_op | source)
XLA Modules:
  0.0 298.7 jit_solution(13508788820080793319)
XLA Ops:
  10.8 1.3 dynamic-slice
  16.0 1.5 fusion.8
  17.6 3.0 %fusion = bf16[128,4096]{1,0:T(8,128)(2,1)} fusion(f32[128,4096]{1,0:T(8,128)S(1)} %fusion.8, bf16[1,4096,128]{2,1,0:T(8,128)(2,1)} %param.16, f32[128,4,128]{0,2,1:T(8,128)} %bitcast.103, f32[4]{0:T(128)S(1)} %get-tuple-element.138, f32[1,4,128,128]{2,3,1,0:T(8,128)S(1)} %get-tuple-element.141, f32[4,128]{1,0:T(4,128)S(1)} %fusion.13, ...), kind=kOutput, calls=%fused_computation.2 | convolution fusion | flops 152387584 | bytes 4722704 | tf_op jit(solution)/shard_map/dot_general | solution.py:86
  20.7 88.5 %all-reduce.3.cloned.1.call-done = bf16[128,4096]{1,0:T(8,128)(2,1)} async-done(((bf16[128,4096]{1,0:T(8,128)(2,1)}), bf16[128,4096]{1,0:T(8,128)(2,1)}) %all-reduce.3.cloned.1.call-update) | async-done | bytes 1048592 | tf_op jit(solution)/shard_map/psum | solution.py:89
  109.2 1.6 convert_convert_fusion
  110.8 14.8 %all-reduce = f32[32]{0:T(128)S(1)} all-reduce(f32[32]{0:T(128)S(1)} %copy-done.5), channel_id=1, replica_groups=mesh['pipe'=64,'tensor'=8] {'tensor'}, use_global_device_ids=true, to_apply=%add | all-reduce | flops 32 | bytes 256
  126.2 95.8 %all-gather.3.cloned.1.call-done = bf16[8192,512]{1,0:T(8,128)(2,1)} async-done(((bf16[128,512]{1,0:T(8,128)(2,1)}), bf16[8192,512]{1,0:T(8,128)(2,1)}) %all-gather.3.cloned.1.call-update) | async-done | bytes 8388624 | tf_op jit(solution)/shard_map/all_gather | solution.py:12
  222.1 68.2 %while.16 = (s32[]{:T(128)}, f32[128,512]{1,0:T(8,128)S(1)}, s32[]{:T(128)}, bf16[64,128,512]{2,1,0:T(8,128)(2,1)}, s32[]{:T(128)}, /*index=5*/s32[]{:T(128)}, s32[]{:T(128)}, s32[]{:T(128)}) while((s32[]{:T(128)}, f32[128,512]{1,0:T(8,128)S(1)}, s32[]{:T(128)}, bf16[64,128,512]{2,1,0:T(8,128)(2,1)}, s32[]{:T(128)}, ...), condition=%wide.region_6.7_spmd.clone, body=%wide.region_5.6_spmd.clone.sunk | while | flops 262152 | bytes 655523 | solution.py:21
  223.1 1.0 add_select_fusion.2
  224.2 1.0 add_select_fusion.2
  225.2 1.0 add_select_fusion.2
  226.3 1.0 add_select_fusion.2
  227.4 1.0 add_select_fusion.2
  228.4 1.0 add_select_fusion.2
  229.5 1.0 add_select_fusion.2
  230.6 1.0 add_select_fusion.2
  231.6 1.0 add_select_fusion.2
  232.7 1.0 add_select_fusion.2
  233.8 1.0 add_select_fusion.2
  234.8 1.0 add_select_fusion.2
  235.9 1.0 add_select_fusion.2
  237.0 1.0 add_select_fusion.2
  238.0 1.0 add_select_fusion.2
  239.1 1.0 add_select_fusion.2
  240.2 1.0 add_select_fusion.2
  241.2 1.0 add_select_fusion.2
  242.3 1.0 add_select_fusion.2
  243.4 1.0 add_select_fusion.2
  244.4 1.0 add_select_fusion.2
  264.7 1.0 add_select_fusion.2
  284.9 1.0 add_select_fusion.2
  290.2 1.6 fusion.17
  (75 shorter events, 49.3 us)
Async XLA Ops:
  7.2 8.8 %copy-start = (bf16[1,4096,128]{2,1,0:T(8,128)(2,1)S(1)}, bf16[1,4096,128]{2,1,0:T(8,128)(2,1)}, u32[]{:S(2)}) copy-start(bf16[1,4096,128]{2,1,0:T(8,128)(2,1)} %param.15) | copy-start | bytes 3145732
  7.2 6.8 %copy-start.3 = (bf16[1,128,128]{2,1,0:T(8,128)(2,1)S(1)}, bf16[1,128,128]{2,1,0:T(8,128)(2,1)}, u32[]{:S(2)}) copy-start(bf16[1,128,128]{2,1,0:T(8,128)(2,1)} %param.13) | copy-start | bytes 98308
  7.2 7.1 %copy-start.2 = (f32[1,4]{1,0:T(1,128)S(1)}, f32[1,4]{1,0:T(1,128)}, u32[]{:S(2)}) copy-start(f32[1,4]{1,0:T(1,128)} %param.17) | copy-start | bytes 52
  7.2 102.0 %all-reduce.3.cloned.1.call-start = ((), (), s32[]{:S(2)}) async-start(), calls=%async_computation | async-start | bytes 2097152 | tf_op jit(solution)/shard_map/psum | solution.py:89
  10.7 2.1 copy-start.1
  14.9 1.1 copy-start.4
  17.6 93.3 %copy-start.5 = (f32[32]{0:T(128)S(1)}, f32[32]{0:T(128)}, u32[]{:S(2)}) copy-start(f32[32]{0:T(128)} %copy-done.4) | copy-start | bytes 388
  20.6 201.4 %all-gather.3.cloned.1.call-start = ((), (), s32[]{:S(2)}) async-start(), calls=%async_computation.1 | async-start | bytes 8519680 | tf_op jit(solution)/shard_map/all_gather | solution.py:12
Sparse Core Ops, SparseCore 0:
  20.8 88.4 all-reduce.2
  113.1 108.8 all-gather.2
where the time goes:
time: 300 us; the launch traced here: 299 us
  waiting for transfers between devices  184 us (61%)
  other arithmetic  71.2 us (24%)
  between operations  15.6 us (5%)
  blocking collectives  14.8 us (5%)
  matrix products  6.74 us (2%)
  local copies, waits for them, and re-layouts  4.12 us (1%)
    all_gather x1, waiting for transfers between devices, prefix(): everything = lax.all_gather(x.astype(jnp.bfloat16), axis)  95.8 us
    psum x1, waiting for transfers between devices, body(): lax.psum(partial_value.astype(jnp.bfloat16), 'tensor').astype(jnp.float32)  88.5 us
    select_n x64, other arithmetic, turn(): return jnp.where(reached, new, before)  66.5 us
    unnamed x1, blocking collectives  14.8 us
  transfers between devices with their start and end apart: 2, of which 2 were waited for; matrix products, arithmetic and copies ran while one was open for 0% of the time, Pallas kernels for 0%

commit v1 on v0

v1 whole, which is shorter than its diff:
```python
import jax
import jax.numpy as jnp
from jax import lax
from jax.experimental import pallas as pl
from jax.experimental.pallas import tpu as pltpu
from jax.sharding import PartitionSpec as P

HEAD = 128
MASKED = 8
SEQ = 128
WIDTH = 4096
HEADS_HERE = 4
PARTS = 8
SHARD = WIDTH // PARTS
EXTRA = 16
WEIGHT_COPIES = 4

LAYERS = ("y", "zh", "core")
TENSOR = ("zl", "x")
GROUP = ("zh", "core")

F32 = jnp.float32
BF16 = jnp.bfloat16


def dot(a, b, a_dim, b_dim):
    return lax.dot_general(a, b, (((a_dim,), (b_dim,)), ((), ())), preferred_element_type=F32)


def front_kernel(
    order_ref, layer_gate_ref, head_gate_ref, q_ref, k_ref, v_ref, grad_ref, kw_ref, vw_ref,
    part_ref, head_grad_ref, kw_buf, vw_buf, sems,
):
    rows = WIDTH // WEIGHT_COPIES
    copies = []
    for i in range(WEIGHT_COPIES):
        span = pl.ds(i * rows, rows)
        pair = (
            pltpu.make_async_copy(kw_ref.at[0, span], kw_buf.at[span], sems.at[0, i]),
            pltpu.make_async_copy(vw_ref.at[0, span], vw_buf.at[span], sems.at[1, i]),
        )
        for copy in pair:
            copy.start()
        copies.append(pair)

    tensor_place = lax.axis_index("zl") * 4 + lax.axis_index("x")
    layer_value = layer_gate_ref[0]
    scale = HEAD ** (-0.5)
    keys = k_ref[0]
    values = v_ref[0]
    key_at = lax.broadcasted_iota(jnp.int32, (SEQ, SEQ), 0)
    query_at = lax.broadcasted_iota(jnp.int32, (SEQ, SEQ), 1)
    seen = key_at <= query_at
    lane = lax.broadcasted_iota(jnp.int32, (1, 128), 1)

    key_grad = jnp.zeros((SEQ, HEAD), F32)
    value_grad = jnp.zeros((SEQ, HEAD), F32)
    head_grads = jnp.zeros((1, 128), F32)
    layer_part = jnp.zeros((1, 1), F32)
    for h in range(HEADS_HERE):
        head_id = tensor_place * HEADS_HERE + h
        masked = order_ref[0, 0] == head_id
        for m in range(1, MASKED):
            masked = jnp.logical_or(masked, order_ref[0, m] == head_id)
        open_gate = jnp.where(masked, 0.0, head_gate_ref[0, h])
        gate = layer_value * open_gate
        span = pl.ds(h * HEAD, HEAD)
        queries = q_ref[0, :, span]
        grads = grad_ref[0, :, span]
        scores = jnp.where(seen, dot(keys, queries, 1, 1) * scale, -1e30)
        expo = jnp.exp(scores - jnp.max(scores, axis=0, keepdims=True))
        probs = expo * (1.0 / jnp.sum(expo, axis=0, keepdims=True))
        probs_half = probs.astype(BF16)
        raw = dot(values, grads, 1, 1)
        head_sum = jnp.sum(
            jnp.sum(probs_half.astype(F32) * raw, axis=0, keepdims=True), axis=1, keepdims=True
        )
        scaled = (grads.astype(F32) * gate).astype(BF16)
        prob_grad = raw * gate
        centre = jnp.sum(probs * prob_grad, axis=0, keepdims=True)
        score_grad = (probs * (prob_grad - centre) * scale).astype(BF16)
        key_grad += dot(score_grad, queries, 1, 0)
        value_grad += dot(probs_half, scaled, 1, 0)
        head_grads += jnp.where(lane == h, layer_value * head_sum, 0.0)
        layer_part += open_gate * head_sum

    head_grad_ref[...] = head_grads[:, :HEADS_HERE]
    both = jnp.concatenate([key_grad.astype(BF16), value_grad.astype(BF16)], axis=1)
    share = jnp.broadcast_to(layer_part, (EXTRA, 128))
    high = share.astype(BF16).astype(F32)
    row = lax.broadcasted_iota(jnp.int32, (EXTRA, 128), 0)
    extra = jnp.where(row < EXTRA // 2, high, share - high).astype(BF16)
    per_copy = PARTS // WEIGHT_COPIES
    for i in range(WEIGHT_COPIES):
        for copy in copies[i]:
            copy.wait()
        for j in range(i * per_copy, (i + 1) * per_copy):
            span = pl.ds(j * SHARD, SHARD)
            weights = jnp.concatenate([kw_buf[span], vw_buf[span]], axis=1)
            part_ref[j, pl.ds(0, SHARD)] = dot(weights, both, 1, 1).astype(BF16)
            part_ref[j, pl.ds(SHARD, EXTRA)] = extra


def front(order, layer_gate, head_gate, q, k, v, grad, kw, vw):
    smem = pl.BlockSpec(memory_space=pltpu.SMEM)
    vmem = pl.BlockSpec(memory_space=pltpu.VMEM)
    hbm = pl.BlockSpec(memory_space=pl.ANY)
    return pl.pallas_call(
        front_kernel,
        name="front",
        out_shape=(
            jax.ShapeDtypeStruct((PARTS, SHARD + EXTRA, SEQ), BF16),
            jax.ShapeDtypeStruct((1, HEADS_HERE), F32),
        ),
        in_specs=[smem, smem, smem, vmem, vmem, vmem, vmem, hbm, hbm],
        out_specs=(vmem, vmem),
        scratch_shapes=[
            pltpu.VMEM((WIDTH, HEAD), BF16),
            pltpu.VMEM((WIDTH, HEAD), BF16),
            pltpu.SemaphoreType.DMA((2, WEIGHT_COPIES)),
        ],
        compiler_params=pltpu.CompilerParams(vmem_limit_bytes=24 * 1024 * 1024),
    )(order, layer_gate, head_gate, q, k, v, grad, kw, vw)


def reduce_kernel(parts_ref, term_ref, layer_grad_ref):
    total = parts_ref[0].astype(F32)
    for j in range(1, PARTS):
        total += parts_ref[j].astype(F32)
    term = total[:SHARD].T.astype(BF16)
    for r in range(PARTS):
        term_ref[r] = term[r * 16:(r + 1) * 16]
    extra = total[SHARD:]
    layer_grad_ref[0] = extra[0, 0] + extra[EXTRA // 2, 0]


def totals_kernel(terms_ref, totals_ref):
    total = terms_ref[0].astype(F32)
    for j in range(1, PARTS):
        total += terms_ref[j].astype(F32)
    total = total.astype(BF16)
    for j in range(PARTS):
        totals_ref[j] = total


def suffix_kernel(terms_ref, totals_ref, out_ref):
    place = lax.axis_index("y")
    running = jnp.zeros(terms_ref.shape[1:], F32)
    for j in range(1, PARTS):
        running += jnp.where(place < j, totals_ref[j].astype(F32), 0.0)
    for j in range(PARTS - 1, -1, -1):
        running += terms_ref[j].astype(F32)
        out_ref[j] = running.astype(BF16)


def small(kernel, name, out_shape, out_specs=None):
    vmem = pl.BlockSpec(memory_space=pltpu.VMEM)
    return pl.pallas_call(
        kernel,
        name=name,
        out_shape=out_shape,
        out_specs=vmem if out_specs is None else out_specs,
        compiler_params=pltpu.CompilerParams(vmem_limit_bytes=16 * 1024 * 1024),
    )


def body(
    queries, keys, values, out_grad, key_weight, value_weight, head_gate, layer_gate, head_order
):
    part, head_grad = front(
        head_order, layer_gate, head_gate, queries, keys, values, out_grad, key_weight, value_weight
    )
    parts = lax.all_to_all(part, TENSOR, 0, 0)
    rows = jax.ShapeDtypeStruct((PARTS, SEQ // PARTS, SHARD), BF16)
    term, layer_grad = small(
        reduce_kernel,
        "reduce_parts",
        (rows, jax.ShapeDtypeStruct((1,), F32)),
        (pl.BlockSpec(memory_space=pltpu.VMEM), pl.BlockSpec(memory_space=pltpu.SMEM)),
    )(parts)
    terms = lax.all_to_all(term, GROUP, 0, 0)
    total = small(totals_kernel, "group_totals", rows)(terms)
    totals = lax.all_to_all(total, "y", 0, 0)
    sums = small(suffix_kernel, "suffix_sums", rows)(terms, totals)
    input_grad = lax.all_to_all(sums, GROUP, 0, 0).reshape(1, SEQ, SHARD)
    return input_grad, head_grad, layer_grad


def solution(mesh):
    fine = jax.sharding.Mesh(mesh.devices.reshape(8, 4, 2, 2, 4), LAYERS + TENSOR)
    rows = P(LAYERS, None, TENSOR)
    return jax.shard_map(
        body,
        mesh=fine,
        in_specs=(rows, rows, rows, rows, rows, rows, P(LAYERS, TENSOR), P(LAYERS), P(LAYERS, None)),
        out_specs=(rows, P(LAYERS, TENSOR), P(LAYERS)),
        check_vma=False,
    )
```

time: 300 us -> 82.6 us (0.28)
  waiting for transfers between devices: 184 us -> 0 us
  other arithmetic: 71.2 us -> 0 us
  blocking collectives: 14.8 us -> 69.1 us
  between operations: 15.6 us -> 1.32 us
  matrix products: 6.74 us -> 0 us
  Pallas kernels: 0 us -> 3.88 us
  local copies, waits for them, and re-layouts: 4.12 us -> 7.73 us
    all_gather x1 -> x0, waiting for transfers between devices: 95.8 us -> none  [prefix(): everything = lax.all_gather(x.astype(jnp.bfloat16), axis)]
    psum x1 -> x0, waiting for transfers between devices: 88.5 us -> none  [body(): lax.psum(partial_value.astype(jnp.bfloat16), 'tensor').astype(jnp.float32)]
    all_to_all x0 -> x4, blocking collectives: none -> 69.1 us  [the longest x1 21.4 us: body(): terms = lax.all_to_all(term, GROUP, 0, 0)]
    select_n x64 -> x0, other arithmetic: 66.5 us -> none  [turn(): return jnp.where(reached, new, before)]
    unnamed x1 -> x0, blocking collectives: 14.8 us -> none
    dot_general x5 -> x0, matrix products: 6.74 us -> none  [the longest x1 3.04 us: body(): lax.dot_general(value_grad, value_rows, contract, preferred_element_type=...]
    unnamed x15 -> x17, local copies, waits for them, and re-layouts: 2.33 us -> 7.73 us
    pallas_call x0 -> x4, Pallas kernels: none -> 3.88 us  [the longest x1 3.11 us: front(): pl.pallas_call(front_kernel, name='front', out_shape=(jax.ShapeDtypeStruc...]
  transfers between devices with their start and end apart: 2 -> 0, of which waited for: 2 -> 0; matrix products, arithmetic and copies ran while one was open for 0% -> 0% of each run, Pallas kernels for 0% -> 0%
where the time goes in v1:
time: 82.6 us; the launch traced here: 82 us
  blocking collectives  69.1 us (84%)
  local copies, waits for them, and re-layouts  7.73 us (9%)
  Pallas kernels  3.88 us (5%)
  between operations  1.32 us (2%)
    all_to_all x1, blocking collectives, body(): terms = lax.all_to_all(term, GROUP, 0, 0)  21.4 us
    all_to_all x1, blocking collectives, body(): parts = lax.all_to_all(part, TENSOR, 0, 0)  19.6 us
    all_to_all x1, blocking collectives, body(): totals = lax.all_to_all(total, 'y', 0, 0)  14.5 us
    all_to_all x1, blocking collectives, body(): input_grad = lax.all_to_all(sums, GROUP, 0, 0).reshape(1, SEQ, SHARD)  13.6 us
    unnamed x17, local copies, waits for them, and re-layouts  7.73 us
    pallas_call x1, Pallas kernels, front(): pl.pallas_call(front_kernel, name='front', out_shape=(jax.ShapeDtypeStruc...  3.11 us

profile of v1, /device:TPU:1, one launch (start us, length us, event | category | flops | bytes accessed | tf_op | source)
XLA Modules:
  0.0 82.0 jit_solution(5379575615938383302)
XLA Ops:
  1.3 0.0 copy-start
  1.3 1.2 %copy-done = bf16[1,4096,128]{2,1,0:T(8,128)(2,1)S(1)} copy-done((bf16[1,4096,128]{2,1,0:T(8,128)(2,1)S(1)}, bf16[1,4096,128]{2,1,0:T(8,128)(2,1)}, u32[]{:S(2)}) %copy-start) | copy-done | bytes 1048600
  2.5 0.0 copy-start.1
  2.5 1.2 %copy-done.1 = bf16[1,4096,128]{2,1,0:T(8,128)(2,1)S(1)} copy-done((bf16[1,4096,128]{2,1,0:T(8,128)(2,1)S(1)}, bf16[1,4096,128]{2,1,0:T(8,128)(2,1)}, u32[]{:S(2)}) %copy-start.1) | copy-done | bytes 1048600
  3.7 0.0 copy-start.2
  3.7 0.9 %copy-done.2 = bf16[1,128,512]{2,1,0:T(8,128)(2,1)S(1)} copy-done((bf16[1,128,512]{2,1,0:T(8,128)(2,1)S(1)}, bf16[1,128,512]{2,1,0:T(8,128)(2,1)}, u32[]{:S(2)}) %copy-start.2) | copy-done | bytes 131096
  4.6 0.0 copy-start.3
  4.6 0.9 %copy-done.3 = bf16[1,128,512]{2,1,0:T(8,128)(2,1)S(1)} copy-done((bf16[1,128,512]{2,1,0:T(8,128)(2,1)S(1)}, bf16[1,128,512]{2,1,0:T(8,128)(2,1)}, u32[]{:S(2)}) %copy-start.3) | copy-done | bytes 131096
  5.5 0.0 copy-start.4
  5.5 0.8 copy-done.4
  6.3 0.0 copy-start.5
  6.3 0.8 copy-done.5
  7.1 0.0 copy-start.6
  7.1 0.7 copy-done.6
  7.7 0.0 copy-start.7
  7.7 0.7 copy-done.7
  8.4 3.1 %front.1 = (bf16[8,528,128]{2,1,0:T(8,128)(2,1)S(1)}, f32[1,4]{1,0:T(1,128)}) custom-call(s32[1,32]{1,0:T(1,128)S(1)} %copy-done.6, f32[1]{0:T(128)S(6)} %copy.13.layer_gate_ref, f32[1,4]{1,0:T(1,128)S(1)} %copy-done.7, bf16[1,128,512]{2,1,0:T(8,128)(2,1)S(1)} %copy-done.2, bf16[1,128,128]{2,1,0:T(8,128)(2,1)S(1)} %copy-done.4, ...), custom_call_target="tpu_custom_call" | custom-call | tf_op jit(solution)/shard_map/front/pallas_call | solution.py:108
  11.5 19.6 %all_to_all.20.parts_ref = bf16[8,528,128]{2,1,0:T(8,128)(2,1)S(1)} all-to-all(bf16[8,528,128]{2,1,0:T(8,128)(2,1)S(1)} %get-tuple-element.7), channel_id=1, replica_groups=mesh['y'=8,'zh'=4,'core'=2,'zl'=2,'x'=4] {'zl','x'}, dimensions={0} | all-to-all | bytes 2162688 | tf_op jit(solution)/shard_map/all_to_all | solution.py:173
  31.1 0.7 reduce_parts.1
  31.8 21.4 %all_to_all.21.terms_ref = bf16[8,16,512]{2,1,0:T(8,128)(2,1)S(1)} all-to-all(bf16[8,16,512]{2,1,0:T(8,128)(2,1)S(1)} %get-tuple-element.8), channel_id=1, replica_groups=mesh['y'=8,'zh'=4,'core'=2,'zl'=2,'x'=4] {'zh','core'}, dimensions={0} | all-to-all | bytes 262144 | tf_op jit(solution)/shard_map/all_to_all | solution.py:181
  53.2 14.5 %all_to_all.22.totals_ref = bf16[8,16,512]{2,1,0:T(8,128)(2,1)S(1)} all-to-all(bf16[8,16,512]{2,1,0:T(8,128)(2,1)S(1)} %group_totals.1), channel_id=1, replica_groups=mesh['y'=8,'zh'=4,'core'=2,'zl'=2,'x'=4] {'y'}, dimensions={0} | all-to-all | bytes 262144 | tf_op jit(solution)/shard_map/all_to_all | solution.py:183
  67.7 0.1 suffix_sums.1
  67.8 13.6 %all_to_all.23 = bf16[8,16,512]{2,1,0:T(8,128)(2,1)S(1)} all-to-all(bf16[8,16,512]{2,1,0:T(8,128)(2,1)S(1)} %suffix_sums.1), channel_id=1, replica_groups=mesh['y'=8,'zh'=4,'core'=2,'zl'=2,'x'=4] {'zh','core'}, dimensions={0} | all-to-all | bytes 262144 | tf_op jit(solution)/shard_map/all_to_all | solution.py:185
  81.4 0.7 copy.14
  (1 shorter events, 0.0 us)
Async XLA Ops:
  1.3 1.2 %copy-start = (bf16[1,4096,128]{2,1,0:T(8,128)(2,1)S(1)}, bf16[1,4096,128]{2,1,0:T(8,128)(2,1)}, u32[]{:S(2)}) copy-start(bf16[1,4096,128]{2,1,0:T(8,128)(2,1)} %kw_ref.1) | copy-start | bytes 3145732
  2.5 1.2 %copy-start.1 = (bf16[1,4096,128]{2,1,0:T(8,128)(2,1)S(1)}, bf16[1,4096,128]{2,1,0:T(8,128)(2,1)}, u32[]{:S(2)}) copy-start(bf16[1,4096,128]{2,1,0:T(8,128)(2,1)} %vw_ref.1) | copy-start | bytes 3145732
  3.7 0.9 %copy-start.2 = (bf16[1,128,512]{2,1,0:T(8,128)(2,1)S(1)}, bf16[1,128,512]{2,1,0:T(8,128)(2,1)}, u32[]{:S(2)}) copy-start(bf16[1,128,512]{2,1,0:T(8,128)(2,1)} %q_ref.1) | copy-start | bytes 393220
  4.6 0.9 %copy-start.3 = (bf16[1,128,512]{2,1,0:T(8,128)(2,1)S(1)}, bf16[1,128,512]{2,1,0:T(8,128)(2,1)}, u32[]{:S(2)}) copy-start(bf16[1,128,512]{2,1,0:T(8,128)(2,1)} %grad_ref.1) | copy-start | bytes 393220
  5.5 0.8 copy-start.4
  6.3 0.8 copy-start.5
  7.1 0.7 copy-start.6
  7.7 0.7 copy-start.7

commit v2 on v1

v2 whole, which is shorter than its diff:
```python
import jax
import jax.numpy as jnp
from jax import lax
from jax.experimental import pallas as pl
from jax.experimental.pallas import tpu as pltpu
from jax.sharding import PartitionSpec as P

HEAD = 128
MASKED = 8
SEQ = 128
WIDTH = 4096
HEADS_HERE = 4
PARTS = 8
NEAR = 4
BLOCKS = PARTS * NEAR
BLOCK = WIDTH // BLOCKS
EXTRA = 8
FAR = 4

MESH_AXES = ("yh", "yl", "zh", "core", "zl", "x")
MESH_SHAPE = (4, 2, 4, 2, 2, 4)
LAYER_AXES = ("yh", "yl", "zh", "core")
TENSOR_AXES = ("zl", "x")
NEAR_AXES = ("core", "yl")

F32 = jnp.float32
BF16 = jnp.bfloat16
MIB = 1024 * 1024


def dot(a, b, a_dim, b_dim):
    return lax.dot_general(a, b, (((a_dim,), (b_dim,)), ((), ())), preferred_element_type=F32)


def front_kernel(
    order_hbm, layer_gate_hbm, head_gate_hbm, q_hbm, k_hbm, v_hbm, grad_hbm, kw_hbm, vw_hbm,
    part_ref, head_grad_ref,
    order_ref, layer_gate_ref, head_gate_ref, q_ref, k_ref, v_ref, grad_ref, kw_ref, vw_ref, sems,
):
    pairs = (
        (k_hbm, k_ref), (q_hbm, q_ref), (v_hbm, v_ref), (grad_hbm, grad_ref),
        (order_hbm, order_ref), (layer_gate_hbm, layer_gate_ref), (head_gate_hbm, head_gate_ref),
        (kw_hbm, kw_ref), (vw_hbm, vw_ref),
    )
    copies = [
        pltpu.make_async_copy(source, target, sems.at[i])
        for i, (source, target) in enumerate(pairs)
    ]
    for copy in copies:
        copy.start()

    tensor_place = lax.axis_index("zl") * 4 + lax.axis_index("x")
    scale = HEAD ** (-0.5)
    heads = range(HEADS_HERE)
    key_at = lax.broadcasted_iota(jnp.int32, (SEQ, SEQ), 0)
    query_at = lax.broadcasted_iota(jnp.int32, (SEQ, SEQ), 1)
    seen = key_at <= query_at
    lane = lax.broadcasted_iota(jnp.int32, (1, 128), 1)

    copies[0].wait()
    copies[1].wait()
    keys = k_ref[0]
    queries = [q_ref[0, :, pl.ds(h * HEAD, HEAD)] for h in heads]
    scores = [jnp.where(seen, dot(keys, queries[h], 1, 1) * scale, -1e30) for h in heads]
    copies[2].wait()
    copies[3].wait()
    values = v_ref[0]
    grads = [grad_ref[0, :, pl.ds(h * HEAD, HEAD)] for h in heads]
    raws = [dot(values, grads[h], 1, 1) for h in heads]
    expos = [jnp.exp(scores[h] - jnp.max(scores[h], axis=0, keepdims=True)) for h in heads]
    probs = [expos[h] * (1.0 / jnp.sum(expos[h], axis=0, keepdims=True)) for h in heads]
    halves = [probs[h].astype(BF16) for h in heads]
    centres = [jnp.sum(probs[h] * raws[h], axis=0, keepdims=True) for h in heads]
    sums = [jnp.sum(halves[h].astype(F32) * raws[h], axis=0, keepdims=True) for h in heads]

    for i in range(4, 7):
        copies[i].wait()
    layer_value = layer_gate_ref[0]
    key_grad = jnp.zeros((SEQ, HEAD), F32)
    value_grad = jnp.zeros((SEQ, HEAD), F32)
    head_grads = jnp.zeros((1, 128), F32)
    layer_part = jnp.zeros((1, 1), F32)
    for h in heads:
        head_id = tensor_place * HEADS_HERE + h
        masked = order_ref[0, 0] == head_id
        for m in range(1, MASKED):
            masked = jnp.logical_or(masked, order_ref[0, m] == head_id)
        open_gate = jnp.where(masked, 0.0, head_gate_ref[0, h])
        gate = layer_value * open_gate
        scaled = (grads[h].astype(F32) * gate).astype(BF16)
        score_grad = (probs[h] * (raws[h] - centres[h]) * (gate * scale)).astype(BF16)
        key_grad += dot(score_grad, queries[h], 1, 0)
        value_grad += dot(halves[h], scaled, 1, 0)
        head_sum = jnp.sum(sums[h], axis=1, keepdims=True)
        head_grads += jnp.where(lane == h, layer_value * head_sum, 0.0)
        layer_part += open_gate * head_sum

    head_grad_ref[...] = head_grads[:, :HEADS_HERE]
    both = jnp.concatenate([key_grad.astype(BF16), value_grad.astype(BF16)], axis=1)
    share = jnp.broadcast_to(layer_part, (EXTRA, 128))
    high = share.astype(BF16).astype(F32)
    row = lax.broadcasted_iota(jnp.int32, (EXTRA, 128), 0)
    extra = jnp.where(row < EXTRA // 2, high, share - high)
    copies[7].wait()
    copies[8].wait()
    for j in range(BLOCKS):
        span = pl.ds(j * BLOCK, BLOCK)
        weights = jnp.concatenate([kw_ref[0, span], vw_ref[0, span]], axis=1)
        part_ref[j] = jnp.concatenate([dot(weights, both, 1, 1), extra], axis=0).astype(BF16)


def front(order, layer_gate, head_gate, q, k, v, grad, kw, vw):
    vmem = pl.BlockSpec(memory_space=pltpu.VMEM)
    hbm = pl.BlockSpec(memory_space=pltpu.HBM)
    return pl.pallas_call(
        front_kernel,
        name="front",
        out_shape=(
            jax.ShapeDtypeStruct((BLOCKS, BLOCK + EXTRA, SEQ), BF16),
            jax.ShapeDtypeStruct((1, HEADS_HERE), F32),
        ),
        in_specs=[hbm] * 9,
        out_specs=(vmem, vmem),
        scratch_shapes=[
            pltpu.SMEM(order.shape, jnp.int32),
            pltpu.SMEM(layer_gate.shape, F32),
            pltpu.SMEM(head_gate.shape, F32),
            pltpu.VMEM(q.shape, BF16),
            pltpu.VMEM(k.shape, BF16),
            pltpu.VMEM(v.shape, BF16),
            pltpu.VMEM(grad.shape, BF16),
            pltpu.VMEM(kw.shape, BF16),
            pltpu.VMEM(vw.shape, BF16),
            pltpu.SemaphoreType.DMA((9,)),
        ],
        compiler_params=pltpu.CompilerParams(vmem_limit_bytes=58 * MIB),
    )(order, layer_gate, head_gate, q, k, v, grad, kw, vw)


def terms_kernel(parts_ref, terms_ref, totals_ref, layer_grad_ref):
    own = lax.axis_index("core") * 2 + lax.axis_index("yl")
    total = jnp.zeros((BLOCK, SEQ), F32)
    share = jnp.zeros((EXTRA, SEQ), F32)
    for n in range(NEAR):
        term = parts_ref[n].astype(F32)
        for t in range(1, PARTS):
            term += parts_ref[t * NEAR + n].astype(F32)
        terms_ref[n] = term[:BLOCK]
        total += term[:BLOCK]
        share += jnp.where(own == n, term[BLOCK:], 0.0)
    total = total.astype(BF16)
    for f in range(FAR):
        totals_ref[f] = total
    layer_grad_ref[0] = share[0, 0] + share[EXTRA // 2, 0]


def later_kernel(terms_ref, totals_ref, later_ref):
    y_place = lax.axis_index("yh")
    z_place = lax.axis_index("zh")
    far = jnp.zeros((BLOCK, SEQ), F32)
    for f in range(1, FAR):
        far += jnp.where(y_place < f, totals_ref[f].astype(F32), 0.0)
    first = terms_ref[0] + terms_ref[2]
    second = terms_ref[1] + terms_ref[3]
    for f in range(FAR):
        ahead = z_place > f
        later_ref[f, 0] = (far + second + jnp.where(ahead, first, 0.0)).astype(BF16)
        later_ref[f, 1] = (far + jnp.where(ahead, second, 0.0)).astype(BF16)


def sums_kernel(terms_ref, later_ref, sums_ref):
    for half in range(2):
        running = later_ref[0, half].astype(F32)
        for f in range(1, FAR):
            running += later_ref[f, half].astype(F32)
        for n in (2 + half, half):
            running += terms_ref[n]
            sums_ref[n] = running.T.astype(BF16)


def join_kernel(blocks_ref, out_ref):
    for n in range(NEAR):
        out_ref[0, :, n * BLOCK:(n + 1) * BLOCK] = blocks_ref[n]


def small(kernel, name, out_shape, out_specs=None):
    vmem = pl.BlockSpec(memory_space=pltpu.VMEM)
    return pl.pallas_call(
        kernel,
        name=name,
        out_shape=out_shape,
        out_specs=vmem if out_specs is None else out_specs,
        compiler_params=pltpu.CompilerParams(vmem_limit_bytes=16 * MIB),
    )


def body(
    queries, keys, values, out_grad, key_weight, value_weight, head_gate, layer_gate, head_order
):
    part, head_grad = front(
        head_order, layer_gate, head_gate, queries, keys, values, out_grad, key_weight, value_weight
    )
    parts = lax.all_to_all(part, TENSOR_AXES + NEAR_AXES, 0, 0)
    vmem = pl.BlockSpec(memory_space=pltpu.VMEM)
    terms, totals, layer_grad = small(
        terms_kernel,
        "terms",
        (
            jax.ShapeDtypeStruct((NEAR, BLOCK, SEQ), F32),
            jax.ShapeDtypeStruct((FAR, BLOCK, SEQ), BF16),
            jax.ShapeDtypeStruct((1,), F32),
        ),
        (vmem, vmem, pl.BlockSpec(memory_space=pltpu.SMEM)),
    )(parts)
    totals = lax.all_to_all(totals, "yh", 0, 0)
    later = small(
        later_kernel, "later", jax.ShapeDtypeStruct((FAR, 2, BLOCK, SEQ), BF16)
    )(terms, totals)
    later = lax.all_to_all(later, "zh", 0, 0)
    sums = small(
        sums_kernel, "sums", jax.ShapeDtypeStruct((NEAR, SEQ, BLOCK), BF16)
    )(terms, later)
    sums = lax.all_to_all(sums, NEAR_AXES, 0, 0)
    input_grad = small(
        join_kernel, "join", jax.ShapeDtypeStruct((1, SEQ, NEAR * BLOCK), BF16)
    )(sums)
    return input_grad, head_grad, layer_grad


def solution(mesh):
    fine = jax.sharding.Mesh(mesh.devices.reshape(MESH_SHAPE), MESH_AXES)
    rows = P(LAYER_AXES, None, TENSOR_AXES)
    heads = P(LAYER_AXES, TENSOR_AXES)
    layers = P(LAYER_AXES)
    return jax.shard_map(
        body,
        mesh=fine,
        in_specs=(rows, rows, rows, rows, rows, rows, heads, layers, P(LAYER_AXES, None)),
        out_specs=(rows, heads, layers),
        check_vma=False,
    )
```

time: 82.6 us -> 73.4 us (0.89)
  local copies, waits for them, and re-layouts: 7.73 us -> 0 us
  blocking collectives: 69.1 us -> 66.7 us
  Pallas kernels: 3.88 us -> 5.08 us
    unnamed x17 -> x0, local copies, waits for them, and re-layouts: 7.73 us -> none
    all_to_all x4, blocking collectives: 69.1 us -> 66.7 us  [the longest x1 28.2 us: body(): parts = lax.all_to_all(part, TENSOR_AXES + NEAR_AXES, 0, 0)]
where the time goes in v2:
time: 73.4 us; the launch traced here: 73 us
  blocking collectives  66.7 us (91%)
  Pallas kernels  5.08 us (7%)
  between operations  1.3 us (2%)
    all_to_all x1, blocking collectives, body(): parts = lax.all_to_all(part, TENSOR_AXES + NEAR_AXES, 0, 0)  28.2 us
    all_to_all x1, blocking collectives, body(): later = lax.all_to_all(later, 'zh', 0, 0)  17.3 us
    all_to_all x1, blocking collectives, body(): totals = lax.all_to_all(totals, 'yh', 0, 0)  11.5 us
    all_to_all x1, blocking collectives, body(): sums = lax.all_to_all(sums, NEAR_AXES, 0, 0)  9.6 us
    pallas_call x1, Pallas kernels, front(): pl.pallas_call(front_kernel, name='front', out_shape=(jax.ShapeDtypeStruc...  3.51 us

profile of v2, /device:TPU:1, one launch (start us, length us, event | category | flops | bytes accessed | tf_op | source)
XLA Modules:
  0.0 73.0 jit_solution(3192655484428957057)
XLA Ops:
  1.3 3.5 %front.1 = (bf16[32,136,128]{2,1,0:T(8,128)(2,1)}, f32[1,4]{1,0:T(1,128)}) custom-call(s32[1,32]{1,0:T(1,128)} %order_hbm.1, f32[1]{0:T(128)S(6)} %copy.12.layer_gate_hbm, f32[1,4]{1,0:T(1,128)} %head_gate_hbm.1, bf16[1,128,512]{2,1,0:T(8,128)(2,1)} %q_hbm.1, bf16[1,128,128]{2,1,0:T(8,128)(2,1)} %k_hbm.1, bf16[1,128,128]{2,1,0:T(8,128)(2,1)} %v_hbm.1, ...), custom_call_target="tpu_custom_call" | custom-call | tf_op jit(solution)/shard_map/front/pallas_call | solution.py:115
  4.8 28.2 %all_to_all.20.parts_ref = bf16[32,136,128]{2,1,0:T(8,128)(2,1)S(1)} all-to-all(bf16[32,136,128]{2,1,0:T(8,128)(2,1)} %get-tuple-element.8), channel_id=1, replica_groups=mesh['yh'=4,'yl'=2,'zh'=4,'core'=2,'zl'=2,'x'=4] {'zl','x','core','yl'}, dimensions={0} | all-to-all | bytes 2228224 | tf_op jit(solution)/shard_map/all_to_all | solution.py:203
  33.0 0.7 terms.1
  33.7 11.5 %all_to_all.21.totals_ref = bf16[4,128,128]{2,1,0:T(8,128)(2,1)S(1)} all-to-all(bf16[4,128,128]{2,1,0:T(8,128)(2,1)S(1)} %get-tuple-element.10), channel_id=1, replica_groups=mesh['yh'=4,'yl'=2,'zh'=4,'core'=2,'zl'=2,'x'=4] {'yh'}, dimensions={0} | all-to-all | bytes 262144 | tf_op jit(solution)/shard_map/all_to_all | solution.py:215
  45.3 0.1 later.1
  45.3 17.3 %all_to_all.22.later_ref = bf16[4,2,128,128]{3,2,1,0:T(8,128)(2,1)S(1)} all-to-all(bf16[4,2,128,128]{3,2,1,0:T(8,128)(2,1)S(1)} %later.1), channel_id=1, replica_groups=mesh['yh'=4,'yl'=2,'zh'=4,'core'=2,'zl'=2,'x'=4] {'zh'}, dimensions={0} | all-to-all | bytes 524288 | tf_op jit(solution)/shard_map/all_to_all | solution.py:219
  62.6 0.1 sums.1
  62.8 9.6 %all_to_all.23.blocks_ref = bf16[4,128,128]{2,1,0:T(8,128)(2,1)S(1)} all-to-all(bf16[4,128,128]{2,1,0:T(8,128)(2,1)S(1)} %sums.1), channel_id=1, replica_groups=mesh['yh'=4,'yl'=2,'zh'=4,'core'=2,'zl'=2,'x'=4] {'core','yl'}, dimensions={0} | all-to-all | bytes 262144 | tf_op jit(solution)/shard_map/all_to_all | solution.py:223
  72.4 0.7 join.1

commit v3 on v2

--- a/solution.py
+++ b/solution.py
@@ -33,13 +33,13 @@
 
 
 def front_kernel(
-    order_hbm, layer_gate_hbm, head_gate_hbm, q_hbm, k_hbm, v_hbm, grad_hbm, kw_hbm, vw_hbm,
-    part_ref, head_grad_ref,
-    order_ref, layer_gate_ref, head_gate_ref, q_ref, k_ref, v_ref, grad_ref, kw_ref, vw_ref, sems,
+    order_hbm, head_gate_hbm, q_hbm, k_hbm, v_hbm, grad_hbm, kw_hbm, vw_hbm,
+    part_ref, head_sum_ref,
+    order_ref, head_gate_ref, q_ref, k_ref, v_ref, grad_ref, kw_ref, vw_ref, sems,
 ):
     pairs = (
         (k_hbm, k_ref), (q_hbm, q_ref), (v_hbm, v_ref), (grad_hbm, grad_ref),
-        (order_hbm, order_ref), (layer_gate_hbm, layer_gate_ref), (head_gate_hbm, head_gate_ref),
+        (order_hbm, order_ref), (head_gate_hbm, head_gate_ref),
         (kw_hbm, kw_ref), (vw_hbm, vw_ref),
     )
     copies = [
@@ -73,12 +73,11 @@
     centres = [jnp.sum(probs[h] * raws[h], axis=0, keepdims=True) for h in heads]
     sums = [jnp.sum(halves[h].astype(F32) * raws[h], axis=0, keepdims=True) for h in heads]
 
-    for i in range(4, 7):
+    for i in range(4, 6):
         copies[i].wait()
-    layer_value = layer_gate_ref[0]
     key_grad = jnp.zeros((SEQ, HEAD), F32)
     value_grad = jnp.zeros((SEQ, HEAD), F32)
-    head_grads = jnp.zeros((1, 128), F32)
+    head_sums = jnp.zeros((1, 128), F32)
     layer_part = jnp.zeros((1, 1), F32)
     for h in heads:
         head_id = tensor_place * HEADS_HERE + h
@@ -86,30 +85,29 @@
         for m in range(1, MASKED):
             masked = jnp.logical_or(masked, order_ref[0, m] == head_id)
         open_gate = jnp.where(masked, 0.0, head_gate_ref[0, h])
-        gate = layer_value * open_gate
-        scaled = (grads[h].astype(F32) * gate).astype(BF16)
-        score_grad = (probs[h] * (raws[h] - centres[h]) * (gate * scale)).astype(BF16)
+        scaled = (grads[h].astype(F32) * open_gate).astype(BF16)
+        score_grad = (probs[h] * (raws[h] - centres[h]) * (open_gate * scale)).astype(BF16)
         key_grad += dot(score_grad, queries[h], 1, 0)
         value_grad += dot(halves[h], scaled, 1, 0)
         head_sum = jnp.sum(sums[h], axis=1, keepdims=True)
-        head_grads += jnp.where(lane == h, layer_value * head_sum, 0.0)
+        head_sums += jnp.where(lane == h, head_sum, 0.0)
         layer_part += open_gate * head_sum
 
-    head_grad_ref[...] = head_grads[:, :HEADS_HERE]
+    head_sum_ref[...] = head_sums
     both = jnp.concatenate([key_grad.astype(BF16), value_grad.astype(BF16)], axis=1)
     share = jnp.broadcast_to(layer_part, (EXTRA, 128))
     high = share.astype(BF16).astype(F32)
     row = lax.broadcasted_iota(jnp.int32, (EXTRA, 128), 0)
     extra = jnp.where(row < EXTRA // 2, high, share - high)
+    copies[6].wait()
     copies[7].wait()
-    copies[8].wait()
     for j in range(BLOCKS):
         span = pl.ds(j * BLOCK, BLOCK)
         weights = jnp.concatenate([kw_ref[0, span], vw_ref[0, span]], axis=1)
         part_ref[j] = jnp.concatenate([dot(weights, both, 1, 1), extra], axis=0).astype(BF16)
 
 
-def front(order, layer_gate, head_gate, q, k, v, grad, kw, vw):
+def front(order, head_gate, q, k, v, grad, kw, vw):
     vmem = pl.BlockSpec(memory_space=pltpu.VMEM)
     hbm = pl.BlockSpec(memory_space=pltpu.HBM)
     return pl.pallas_call(
@@ -117,13 +115,12 @@
         name="front",
         out_shape=(
             jax.ShapeDtypeStruct((BLOCKS, BLOCK + EXTRA, SEQ), BF16),
-            jax.ShapeDtypeStruct((1, HEADS_HERE), F32),
+            jax.ShapeDtypeStruct((1, 128), F32),
         ),
-        in_specs=[hbm] * 9,
+        in_specs=[hbm] * 8,
         out_specs=(vmem, vmem),
         scratch_shapes=[
             pltpu.SMEM(order.shape, jnp.int32),
-            pltpu.SMEM(layer_gate.shape, F32),
             pltpu.SMEM(head_gate.shape, F32),
             pltpu.VMEM(q.shape, BF16),
             pltpu.VMEM(k.shape, BF16),
@@ -131,13 +128,13 @@
             pltpu.VMEM(grad.shape, BF16),
             pltpu.VMEM(kw.shape, BF16),
             pltpu.VMEM(vw.shape, BF16),
-            pltpu.SemaphoreType.DMA((9,)),
+            pltpu.SemaphoreType.DMA((8,)),
         ],
         compiler_params=pltpu.CompilerParams(vmem_limit_bytes=58 * MIB),
-    )(order, layer_gate, head_gate, q, k, v, grad, kw, vw)
-
-
-def terms_kernel(parts_ref, terms_ref, totals_ref, layer_grad_ref):
+    )(order, head_gate, q, k, v, grad, kw, vw)
+
+
+def terms_kernel(parts_ref, own_gate_ref, y_gate_ref, core_gate_ref, both_gate_ref, terms_ref, totals_ref, share_ref):
     own = lax.axis_index("core") * 2 + lax.axis_index("yl")
     total = jnp.zeros((BLOCK, SEQ), F32)
     share = jnp.zeros((EXTRA, SEQ), F32)
@@ -145,21 +142,27 @@
         term = parts_ref[n].astype(F32)
         for t in range(1, PARTS):
             term += parts_ref[t * NEAR + n].astype(F32)
-        terms_ref[n] = term[:BLOCK]
-        total += term[:BLOCK]
+        apart = own ^ n
+        gate = jnp.where(
+            apart == 0,
+            own_gate_ref[...],
+            jnp.where(
+                apart == 1,
+                y_gate_ref[...],
+                jnp.where(apart == 2, core_gate_ref[...], both_gate_ref[...]),
+            ),
+        )
+        scaled = term[:BLOCK] * gate[:1]
+        terms_ref[n] = scaled
+        total += scaled
         share += jnp.where(own == n, term[BLOCK:], 0.0)
-    total = total.astype(BF16)
-    for f in range(FAR):
-        totals_ref[f] = total
-    layer_grad_ref[0] = share[0, 0] + share[EXTRA // 2, 0]
-
-
-def later_kernel(terms_ref, totals_ref, later_ref):
-    y_place = lax.axis_index("yh")
+    totals_ref[...] = total.astype(BF16)
+    share_ref[...] = share
+
+
+def later_kernel(terms_ref, far_1, far_2, far_3, later_ref):
     z_place = lax.axis_index("zh")
-    far = jnp.zeros((BLOCK, SEQ), F32)
-    for f in range(1, FAR):
-        far += jnp.where(y_place < f, totals_ref[f].astype(F32), 0.0)
+    far = far_1[...].astype(F32) + far_2[...].astype(F32) + far_3[...].astype(F32)
     first = terms_ref[0] + terms_ref[2]
     second = terms_ref[1] + terms_ref[3]
     for f in range(FAR):
@@ -178,7 +181,9 @@
             sums_ref[n] = running.T.astype(BF16)
 
 
-def join_kernel(blocks_ref, out_ref):
+def join_kernel(blocks_ref, share_ref, gate_ref, head_sum_ref, out_ref, head_grad_ref, layer_grad_ref):
+    head_grad_ref[...] = (gate_ref[:1] * head_sum_ref[...])[:, :HEADS_HERE]
+    layer_grad_ref[0] = share_ref[0, 0] + share_ref[EXTRA // 2, 0]
     for n in range(NEAR):
         out_ref[0, :, n * BLOCK:(n + 1) * BLOCK] = blocks_ref[n]
 
@@ -197,33 +202,48 @@
 def body(
     queries, keys, values, out_grad, key_weight, value_weight, head_gate, layer_gate, head_order
 ):
-    part, head_grad = front(
-        head_order, layer_gate, head_gate, queries, keys, values, out_grad, key_weight, value_weight
-    )
+    part, head_sum = front(
+        head_order, head_gate, queries, keys, values, out_grad, key_weight, value_weight
+    )
+    part, layer_gate = lax.optimization_barrier((part, layer_gate))
     parts = lax.all_to_all(part, TENSOR_AXES + NEAR_AXES, 0, 0)
+    gate = jnp.broadcast_to(layer_gate[:, None], (EXTRA, SEQ))
+    swap = ((0, 1), (1, 0))
+    core_gate = lax.ppermute(gate, "core", swap)
+    y_gate = lax.ppermute(gate, "yl", swap)
+    both_gate = lax.ppermute(core_gate, "yl", swap)
     vmem = pl.BlockSpec(memory_space=pltpu.VMEM)
-    terms, totals, layer_grad = small(
+    terms, totals, share = small(
         terms_kernel,
         "terms",
         (
             jax.ShapeDtypeStruct((NEAR, BLOCK, SEQ), F32),
-            jax.ShapeDtypeStruct((FAR, BLOCK, SEQ), BF16),
-            jax.ShapeDtypeStruct((1,), F32),
+            jax.ShapeDtypeStruct((BLOCK, SEQ), BF16),
+            jax.ShapeDtypeStruct((EXTRA, SEQ), F32),
         ),
-        (vmem, vmem, pl.BlockSpec(memory_space=pltpu.SMEM)),
-    )(parts)
-    totals = lax.all_to_all(totals, "yh", 0, 0)
+        (vmem, vmem, vmem),
+    )(parts, gate, y_gate, core_gate, both_gate)
+    totals = [
+        lax.ppermute(totals, "yh", [(f, f - step) for f in range(step, FAR)]) for step in (3, 2, 1)
+    ]
     later = small(
         later_kernel, "later", jax.ShapeDtypeStruct((FAR, 2, BLOCK, SEQ), BF16)
-    )(terms, totals)
+    )(terms, *totals)
     later = lax.all_to_all(later, "zh", 0, 0)
     sums = small(
         sums_kernel, "sums", jax.ShapeDtypeStruct((NEAR, SEQ, BLOCK), BF16)
     )(terms, later)
     sums = lax.all_to_all(sums, NEAR_AXES, 0, 0)
-    input_grad = small(
-        join_kernel, "join", jax.ShapeDtypeStruct((1, SEQ, NEAR * BLOCK), BF16)
-    )(sums)
+    input_grad, head_grad, layer_grad = small(
+        join_kernel,
+        "join",
+        (
+            jax.ShapeDtypeStruct((1, SEQ, NEAR * BLOCK), BF16),
+            jax.ShapeDtypeStruct((1, HEADS_HERE), F32),
+            jax.ShapeDtypeStruct((1,), F32),
+        ),
+        (vmem, vmem, pl.BlockSpec(memory_space=pltpu.SMEM)),
+    )(sums, share, gate, head_sum)
     return input_grad, head_grad, layer_grad
 
 

time: 73.4 us -> 69.1 us (0.941)
  blocking collectives: 66.7 us -> 25.6 us
  starting transfers between devices: 0 us -> 21.9 us
  waiting for transfers between devices: 0 us -> 14.9 us
    all_to_all x2 -> x0, blocking collectives: 39.7 us -> none  [the longest x1 28.2 us: body(): parts = lax.all_to_all(part, TENSOR_AXES + NEAR_AXES, 0, 0)]
    ppermute x0 -> x6, waiting for transfers between devices: none -> 12.2 us  [the longest x3 6.07 us: body(): lax.ppermute(totals, 'yh', [(f, f - step) for f in range(step, FAR)])]
    ppermute x0 -> x6, starting transfers between devices: none -> 11.4 us  [the longest x3 3.88 us: body(): lax.ppermute(totals, 'yh', [(f, f - step) for f in range(step, FAR)])]
    all_to_all x0 -> x1, starting transfers between devices: none -> 10.5 us  [body(): parts = lax.all_to_all(part, TENSOR_AXES + NEAR_AXES, 0, 0)]
    all_to_all x0 -> x1, waiting for transfers between devices: none -> 2.73 us  [body(): parts = lax.all_to_all(part, TENSOR_AXES + NEAR_AXES, 0, 0)]
    all_to_all x1, blocking collectives: 17.3 us -> 15.6 us  [body(): later = lax.all_to_all(later, 'zh', 0, 0)]
  transfers between devices with their start and end apart: 0 -> 7, of which waited for: 0 -> 5; matrix products, arithmetic and copies ran while one was open for 0% -> 0% of each run, Pallas kernels for 0% -> 0%
where the time goes in v3:
time: 69.1 us; the launch traced here: 68.4 us
  blocking collectives  25.6 us (37%)
  starting transfers between devices  21.9 us (32%)
  waiting for transfers between devices  14.9 us (22%)
  Pallas kernels  4.53 us (7%)
  between operations  1.38 us (2%)
    all_to_all x1, blocking collectives, body(): later = lax.all_to_all(later, 'zh', 0, 0)  15.6 us
    all_to_all x1, starting transfers between devices, body(): parts = lax.all_to_all(part, TENSOR_AXES + NEAR_AXES, 0, 0)  10.5 us
    all_to_all x1, blocking collectives, body(): sums = lax.all_to_all(sums, NEAR_AXES, 0, 0)  10.1 us
    ppermute x3, waiting for transfers between devices, body(): lax.ppermute(totals, 'yh', [(f, f - step) for f in range(step, FAR)])  6.07 us
    ppermute x1, waiting for transfers between devices, body(): y_gate = lax.ppermute(gate, 'yl', swap)  6.04 us
    ppermute x3, starting transfers between devices, body(): lax.ppermute(totals, 'yh', [(f, f - step) for f in range(step, FAR)])  3.88 us
    pallas_call x1, Pallas kernels, front(): pl.pallas_call(front_kernel, name='front', out_shape=(jax.ShapeDtypeStruc...  3.5 us
    ppermute x1, starting transfers between devices, body(): y_gate = lax.ppermute(gate, 'yl', swap)  3.31 us
  transfers between devices with their start and end apart: 7, of which 5 were waited for; matrix products, arithmetic and copies ran while one was open for 0% of the time, Pallas kernels for 0%

profile of v3, /device:TPU:1, one launch (start us, length us, event | category | flops | bytes accessed | tf_op | source)
XLA Modules:
  0.0 68.4 jit_solution(3496199246505424282)
XLA Ops:
  0.6 3.5 %front.1 = (bf16[32,136,128]{2,1,0:T(8,128)(2,1)}, f32[1,128]{1,0:T(1,128)}) custom-call(s32[1,32]{1,0:T(1,128)} %order_hbm.1, f32[1,4]{1,0:T(1,128)} %head_gate_hbm.1, bf16[1,128,512]{2,1,0:T(8,128)(2,1)} %q_hbm.1, bf16[1,128,128]{2,1,0:T(8,128)(2,1)} %k_hbm.1, bf16[1,128,128]{2,1,0:T(8,128)(2,1)} %v_hbm.1, bf16[1,128,512]{2,1,0:T(8,128)(2,1)} %grad_hbm.1, ...), custom_call_target="tpu_custom_call" | custom-call | tf_op jit(solution)/shard_map/front/pallas_call | solution.py:113
  4.1 10.5 %all-to-all-start = ((bf16[32,136,128]{2,1,0:T(8,128)(2,1)}), bf16[32,136,128]{2,1,0:T(8,128)(2,1)S(1)}, u32[]{:S(2)}, u32[]{:S(2)}) async-start(bf16[32,136,128]{2,1,0:T(8,128)(2,1)} %get-tuple-element.11), calls=%async_computation | async-start | bytes 2228224 | tf_op jit(solution)/shard_map/all_to_all | solution.py:209
  15.3 2.2 %collective-permute-start.1 = (f32[8,128]{1,0:T(8,128)S(1)}, f32[8,128]{1,0:T(8,128)S(1)}, u32[]{:S(2)}, u32[]{:S(2)}) collective-permute-start(f32[8,128]{1,0:T(8,128)S(1)} %broadcast_in_dim.9.own_gate_ref.gate_ref), channel_id=1, source_target_pairs={{0,8},{8,0},{1,9},{9,1},{2,10},{10,2},{3,11},{11,3},{4,12},{12,4},... | collective-permute-start | bytes 12296 | tf_op jit(solution)/shard_map/ppermute | solution.py:212
  17.6 3.3 %collective-permute-start = (f32[8,128]{1,0:T(8,128)S(1)}, f32[8,128]{1,0:T(8,128)S(1)}, u32[]{:S(2)}, u32[]{:S(2)}) collective-permute-start(f32[8,128]{1,0:T(8,128)S(1)} %broadcast_in_dim.9.own_gate_ref.gate_ref), channel_id=1, source_target_pairs={{0,64},{64,0},{1,65},{65,1},{2,66},{66,2},{3,67},{67,3},{4,68},{68... | collective-permute-start | bytes 12296 | tf_op jit(solution)/shard_map/ppermute | solution.py:213
  20.9 0.0 collective-permute-done.1.core_gate_ref
  20.9 2.0 %collective-permute-start.2 = (f32[8,128]{1,0:T(8,128)S(1)}, f32[8,128]{1,0:T(8,128)S(1)}, u32[]{:S(2)}, u32[]{:S(2)}) collective-permute-start(f32[8,128]{1,0:T(8,128)S(1)} %collective-permute-done.1.core_gate_ref), channel_id=1, source_target_pairs={{0,64},{64,0},{1,65},{65,1},{2,66},{66,2},{3,67},{67,3},{4,68},{68... | collective-permute-start | bytes 12296 | tf_op jit(solution)/shard_map/ppermute | solution.py:214
  22.9 6.0 %collective-permute-done.y_gate_ref = f32[8,128]{1,0:T(8,128)S(1)} collective-permute-done((f32[8,128]{1,0:T(8,128)S(1)}, f32[8,128]{1,0:T(8,128)S(1)}, u32[]{:S(2)}, u32[]{:S(2)}) %collective-permute-start) | collective-permute-done | bytes 4128 | tf_op jit(solution)/shard_map/ppermute | solution.py:213
  28.9 0.1 collective-permute-done.2.both_gate_ref
  29.0 2.7 %all-to-all-done.parts_ref = bf16[32,136,128]{2,1,0:T(8,128)(2,1)S(1)} async-done(((bf16[32,136,128]{2,1,0:T(8,128)(2,1)}), bf16[32,136,128]{2,1,0:T(8,128)(2,1)S(1)}, u32[]{:S(2)}, u32[]{:S(2)}) %all-to-all-start) | async-done | bytes 1114144 | tf_op jit(solution)/shard_map/all_to_all | solution.py:209
  31.7 0.2 terms.1
  31.9 0.0 copy-start
  31.9 1.3 %collective-permute-start.3 = (bf16[128,128]{1,0:T(8,128)(2,1)S(1)}, bf16[128,128]{1,0:T(8,128)(2,1)S(1)}, u32[]{:S(2)}, u32[]{:S(2)}) collective-permute-start(bf16[128,128]{1,0:T(8,128)(2,1)S(1)} %get-tuple-element.14), channel_id=1, source_target_pairs={{384,0},{385,1},{386,2},{387,3},{388,4},{389,5},{390,6},{391,7},{3... | collective-permute-start | bytes 98312 | tf_op jit(solution)/shard_map/ppermute | solution.py:227
  33.2 1.3 %collective-permute-start.4 = (bf16[128,128]{1,0:T(8,128)(2,1)S(1)}, bf16[128,128]{1,0:T(8,128)(2,1)S(1)}, u32[]{:S(2)}, u32[]{:S(2)}) collective-permute-start(bf16[128,128]{1,0:T(8,128)(2,1)S(1)} %get-tuple-element.14), channel_id=1, source_target_pairs={{256,0},{384,128},{257,1},{385,129},{258,2},{386,130},{259,3},{387... | collective-permute-start | bytes 98312 | tf_op jit(solution)/shard_map/ppermute | solution.py:227
  34.5 1.3 %collective-permute-start.5 = (bf16[128,128]{1,0:T(8,128)(2,1)S(1)}, bf16[128,128]{1,0:T(8,128)(2,1)S(1)}, u32[]{:S(2)}, u32[]{:S(2)}) collective-permute-start(bf16[128,128]{1,0:T(8,128)(2,1)S(1)} %get-tuple-element.14), channel_id=1, source_target_pairs={{128,0},{256,128},{384,256},{129,1},{257,129},{385,257},{130,2},{2... | collective-permute-start | bytes 98312 | tf_op jit(solution)/shard_map/ppermute | solution.py:227
  35.8 2.9 %collective-permute-done.3.far_1 = bf16[128,128]{1,0:T(8,128)(2,1)S(1)} collective-permute-done((bf16[128,128]{1,0:T(8,128)(2,1)S(1)}, bf16[128,128]{1,0:T(8,128)(2,1)S(1)}, u32[]{:S(2)}, u32[]{:S(2)}) %collective-permute-start.3) | collective-permute-done | bytes 32800 | tf_op jit(solution)/shard_map/ppermute | solution.py:227
  38.7 3.2 %collective-permute-done.4.far_2 = bf16[128,128]{1,0:T(8,128)(2,1)S(1)} collective-permute-done((bf16[128,128]{1,0:T(8,128)(2,1)S(1)}, bf16[128,128]{1,0:T(8,128)(2,1)S(1)}, u32[]{:S(2)}, u32[]{:S(2)}) %collective-permute-start.4) | collective-permute-done | bytes 32800 | tf_op jit(solution)/shard_map/ppermute | solution.py:227
  41.9 0.0 collective-permute-done.5.far_3
  41.9 0.1 later.1
  41.9 15.6 %all_to_all.15.later_ref = bf16[4,2,128,128]{3,2,1,0:T(8,128)(2,1)S(1)} all-to-all(bf16[4,2,128,128]{3,2,1,0:T(8,128)(2,1)S(1)} %later.1), channel_id=1, replica_groups=mesh['yh'=4,'yl'=2,'zh'=4,'core'=2,'zl'=2,'x'=4] {'zh'}, dimensions={0} | all-to-all | bytes 524288 | tf_op jit(solution)/shard_map/all_to_all | solution.py:232
  57.5 0.1 sums.1
  57.6 10.1 %all_to_all.16.blocks_ref = bf16[4,128,128]{2,1,0:T(8,128)(2,1)S(1)} all-to-all(bf16[4,128,128]{2,1,0:T(8,128)(2,1)S(1)} %sums.1), channel_id=1, replica_groups=mesh['yh'=4,'yl'=2,'zh'=4,'core'=2,'zl'=2,'x'=4] {'core','yl'}, dimensions={0} | all-to-all | bytes 262144 | tf_op jit(solution)/shard_map/all_to_all | solution.py:236
  67.7 0.0 copy-done
  67.7 0.7 %join.1 = (bf16[1,128,512]{2,1,0:T(8,128)(2,1)}, f32[1,4]{1,0:T(1,128)}, f32[1]{0:T(128)}) custom-call(bf16[4,128,128]{2,1,0:T(8,128)(2,1)S(1)} %all_to_all.16.blocks_ref, f32[8,128]{1,0:T(8,128)S(1)} %get-tuple-element.15.share_ref, f32[8,128]{1,0:T(8,128)S(1)} %broadcast_in_dim.9.own_gate_ref.gate_ref, f32[1,128]{1,0:T(1,128)S(1)} %copy-done), custom_call_target="tpu_custom_call" | custom-call | tf_op jit(solution)/shard_map/join/pallas_call | solution.py:237
  (1 shorter events, 0.0 us)
Async XLA Ops:
  4.1 27.6 %all-to-all-start = ((bf16[32,136,128]{2,1,0:T(8,128)(2,1)}), bf16[32,136,128]{2,1,0:T(8,128)(2,1)S(1)}, u32[]{:S(2)}, u32[]{:S(2)}) async-start(bf16[32,136,128]{2,1,0:T(8,128)(2,1)} %get-tuple-element.11), calls=%async_computation | async-start | bytes 2228224 | tf_op jit(solution)/shard_map/all_to_all | solution.py:209
  15.3 5.6 %collective-permute-start.1 = (f32[8,128]{1,0:T(8,128)S(1)}, f32[8,128]{1,0:T(8,128)S(1)}, u32[]{:S(2)}, u32[]{:S(2)}) collective-permute-start(f32[8,128]{1,0:T(8,128)S(1)} %broadcast_in_dim.9.own_gate_ref.gate_ref), channel_id=1, source_target_pairs={{0,8},{8,0},{1,9},{9,1},{2,10},{10,2},{3,11},{11,3},{4,12},{12,4},... | collective-permute-start | bytes 12296 | tf_op jit(solution)/shard_map/ppermute | solution.py:212
  17.6 11.3 %collective-permute-start = (f32[8,128]{1,0:T(8,128)S(1)}, f32[8,128]{1,0:T(8,128)S(1)}, u32[]{:S(2)}, u32[]{:S(2)}) collective-permute-start(f32[8,128]{1,0:T(8,128)S(1)} %broadcast_in_dim.9.own_gate_ref.gate_ref), channel_id=1, source_target_pairs={{0,64},{64,0},{1,65},{65,1},{2,66},{66,2},{3,67},{67,3},{4,68},{68... | collective-permute-start | bytes 12296 | tf_op jit(solution)/shard_map/ppermute | solution.py:213
  20.9 8.1 %collective-permute-start.2 = (f32[8,128]{1,0:T(8,128)S(1)}, f32[8,128]{1,0:T(8,128)S(1)}, u32[]{:S(2)}, u32[]{:S(2)}) collective-permute-start(f32[8,128]{1,0:T(8,128)S(1)} %collective-permute-done.1.core_gate_ref), channel_id=1, source_target_pairs={{0,64},{64,0},{1,65},{65,1},{2,66},{66,2},{3,67},{67,3},{4,68},{68... | collective-permute-start | bytes 12296 | tf_op jit(solution)/shard_map/ppermute | solution.py:214
  31.9 35.8 %copy-start = (f32[1,128]{1,0:T(1,128)S(1)}, f32[1,128]{1,0:T(1,128)}, u32[]{:S(2)}) copy-start(f32[1,128]{1,0:T(1,128)} %get-tuple-element.16.head_sum_ref) | copy-start | bytes 1540
  31.9 6.8 %collective-permute-start.3 = (bf16[128,128]{1,0:T(8,128)(2,1)S(1)}, bf16[128,128]{1,0:T(8,128)(2,1)S(1)}, u32[]{:S(2)}, u32[]{:S(2)}) collective-permute-start(bf16[128,128]{1,0:T(8,128)(2,1)S(1)} %get-tuple-element.14), channel_id=1, source_target_pairs={{384,0},{385,1},{386,2},{387,3},{388,4},{389,5},{390,6},{391,7},{3... | collective-permute-start | bytes 98312 | tf_op jit(solution)/shard_map/ppermute | solution.py:227
  33.2 8.7 %collective-permute-start.4 = (bf16[128,128]{1,0:T(8,128)(2,1)S(1)}, bf16[128,128]{1,0:T(8,128)(2,1)S(1)}, u32[]{:S(2)}, u32[]{:S(2)}) collective-permute-start(bf16[128,128]{1,0:T(8,128)(2,1)S(1)} %get-tuple-element.14), channel_id=1, source_target_pairs={{256,0},{384,128},{257,1},{385,129},{258,2},{386,130},{259,3},{387... | collective-permute-start | bytes 98312 | tf_op jit(solution)/shard_map/ppermute | solution.py:227
  34.5 7.4 %collective-permute-start.5 = (bf16[128,128]{1,0:T(8,128)(2,1)S(1)}, bf16[128,128]{1,0:T(8,128)(2,1)S(1)}, u32[]{:S(2)}, u32[]{:S(2)}) collective-permute-start(bf16[128,128]{1,0:T(8,128)(2,1)S(1)} %get-tuple-element.14), channel_id=1, source_target_pairs={{128,0},{256,128},{384,256},{129,1},{257,129},{385,257},{130,2},{2... | collective-permute-start | bytes 98312 | tf_op jit(solution)/shard_map/ppermute | solution.py:227

commit v4 on v3

--- a/solution.py
+++ b/solution.py
@@ -16,6 +16,12 @@
 BLOCK = WIDTH // BLOCKS
 EXTRA = 8
 FAR = 4
+STEP_1 = ((3, 0), (2, 1))
+STEP_2 = ((2, 0), (3, 1))
+STEP_3 = ((0, 1), (1, 0))
+STEP_4 = ((1, 2), (2, 3))
+STEP_5 = ((3, 2), (1, 3))
+STEP_6 = ((0, 3),)
 
 MESH_AXES = ("yh", "yl", "zh", "core", "zl", "x")
 MESH_SHAPE = (4, 2, 4, 2, 2, 4)
@@ -160,22 +166,34 @@
     share_ref[...] = share
 
 
-def later_kernel(terms_ref, far_1, far_2, far_3, later_ref):
-    z_place = lax.axis_index("zh")
+def later_kernel(
+    terms_ref, far_1, far_2, far_3, own_ref, to_earlier_ref, first_later_ref, second_later_ref
+):
+    place = lax.axis_index("zh")
     far = far_1[...].astype(F32) + far_2[...].astype(F32) + far_3[...].astype(F32)
     first = terms_ref[0] + terms_ref[2]
     second = terms_ref[1] + terms_ref[3]
-    for f in range(FAR):
-        ahead = z_place > f
-        later_ref[f, 0] = (far + second + jnp.where(ahead, first, 0.0)).astype(BF16)
-        later_ref[f, 1] = (far + jnp.where(ahead, second, 0.0)).astype(BF16)
-
-
-def sums_kernel(terms_ref, later_ref, sums_ref):
+    to_later = (far + second, far)
+    to_earlier = (far + second + first, far + second)
     for half in range(2):
-        running = later_ref[0, half].astype(F32)
-        for f in range(1, FAR):
-            running += later_ref[f, half].astype(F32)
+        own_ref[half] = to_later[half]
+        to_earlier_ref[half] = to_earlier[half].astype(BF16)
+        for z, ref in ((0, first_later_ref), (1, second_later_ref)):
+            ref[half] = jnp.where(place == z, to_later[half], to_earlier[half]).astype(BF16)
+
+
+def pass_on_kernel(own_ref, step_1, step_2, step_3, sum_ref, passed_ref):
+    second_place = lax.axis_index("zh") == 1
+    own = own_ref[...]
+    got = step_3[...].astype(F32)
+    passed_ref[...] = (own + jnp.where(second_place, got, 0.0)).astype(BF16)
+    sum_ref[...] = own + got + step_1[...].astype(F32) + step_2[...].astype(F32)
+
+
+def sums_kernel(terms_ref, sum_ref, step_5, step_6, step_4, sums_ref):
+    for half in range(2):
+        running = sum_ref[half] + step_5[half].astype(F32)
+        running += step_6[half].astype(F32) + step_4[half].astype(F32)
         for n in (2 + half, half):
             running += terms_ref[n]
             sums_ref[n] = running.T.astype(BF16)
@@ -226,13 +244,33 @@
     totals = [
         lax.ppermute(totals, "yh", [(f, f - step) for f in range(step, FAR)]) for step in (3, 2, 1)
     ]
-    later = small(
-        later_kernel, "later", jax.ShapeDtypeStruct((FAR, 2, BLOCK, SEQ), BF16)
+    half_pair = (2, BLOCK, SEQ)
+    own, to_earlier, first_later, second_later = small(
+        later_kernel,
+        "later",
+        (
+            jax.ShapeDtypeStruct(half_pair, F32),
+            jax.ShapeDtypeStruct(half_pair, BF16),
+            jax.ShapeDtypeStruct(half_pair, BF16),
+            jax.ShapeDtypeStruct(half_pair, BF16),
+        ),
+        (vmem,) * 4,
     )(terms, *totals)
-    later = lax.all_to_all(later, "zh", 0, 0)
+    step_1 = lax.ppermute(to_earlier, "zh", STEP_1)
+    step_2 = lax.ppermute(to_earlier, "zh", STEP_2)
+    step_3 = lax.ppermute(first_later, "zh", STEP_3)
+    own, passed = small(
+        pass_on_kernel,
+        "pass_on",
+        (jax.ShapeDtypeStruct(half_pair, F32), jax.ShapeDtypeStruct(half_pair, BF16)),
+        (vmem,) * 2,
+    )(own, step_1, step_2, step_3)
+    step_5 = lax.ppermute(second_later, "zh", STEP_5)
+    step_6 = lax.ppermute(first_later, "zh", STEP_6)
+    step_4 = lax.ppermute(passed, "zh", STEP_4)
     sums = small(
         sums_kernel, "sums", jax.ShapeDtypeStruct((NEAR, SEQ, BLOCK), BF16)
-    )(terms, later)
+    )(terms, own, step_5, step_6, step_4)
     sums = lax.all_to_all(sums, NEAR_AXES, 0, 0)
     input_grad, head_grad, layer_grad = small(
         join_kernel,

time: 69.1 us -> 66.5 us (0.962)
  blocking collectives: 25.6 us -> 10.6 us
  starting transfers between devices: 21.9 us -> 34.3 us
    all_to_all x1 -> x0, blocking collectives: 15.6 us -> none  [body(): later = lax.all_to_all(later, 'zh', 0, 0)]
    ppermute x0 -> x6, starting transfers between devices: none -> 12.4 us  [the longest x1 4.62 us: body(): step_6 = lax.ppermute(first_later, 'zh', STEP_6)]
  transfers between devices with their start and end apart: 7 -> 13, of which waited for: 5 -> 5; matrix products, arithmetic and copies ran while one was open for 0% -> 0% of each run, Pallas kernels for 0% -> 0%
where the time goes in v4:
time: 66.5 us; the launch traced here: 65.9 us
  starting transfers between devices  34.3 us (52%)
  waiting for transfers between devices  14.9 us (22%)
  blocking collectives  10.6 us (16%)
  Pallas kernels  4.58 us (7%)
  between operations  1.48 us (2%)
    all_to_all x1, blocking collectives, body(): sums = lax.all_to_all(sums, NEAR_AXES, 0, 0)  10.6 us
    all_to_all x1, starting transfers between devices, body(): parts = lax.all_to_all(part, TENSOR_AXES + NEAR_AXES, 0, 0)  10.5 us
    ppermute x3, waiting for transfers between devices, body(): lax.ppermute(totals, 'yh', [(f, f - step) for f in range(step, FAR)])  6.07 us
    ppermute x1, waiting for transfers between devices, body(): y_gate = lax.ppermute(gate, 'yl', swap)  6.04 us
    ppermute x1, starting transfers between devices, body(): step_6 = lax.ppermute(first_later, 'zh', STEP_6)  4.62 us
    ppermute x1, starting transfers between devices, body(): step_3 = lax.ppermute(first_later, 'zh', STEP_3)  3.9 us
    ppermute x3, starting transfers between devices, body(): lax.ppermute(totals, 'yh', [(f, f - step) for f in range(step, FAR)])  3.88 us
    pallas_call x1, Pallas kernels, front(): pl.pallas_call(front_kernel, name='front', out_shape=(jax.ShapeDtypeStruc...  3.52 us
  transfers between devices with their start and end apart: 13, of which 5 were waited for; matrix products, arithmetic and copies ran while one was open for 0% of the time, Pallas kernels for 0%

profile of v4, /device:TPU:1, one launch (start us, length us, event | category | flops | bytes accessed | tf_op | source)
XLA Modules:
  0.0 65.9 jit_solution(17767259544641474292)
XLA Ops:
  0.6 3.5 %front.1 = (bf16[32,136,128]{2,1,0:T(8,128)(2,1)}, f32[1,128]{1,0:T(1,128)}) custom-call(s32[1,32]{1,0:T(1,128)} %order_hbm.1, f32[1,4]{1,0:T(1,128)} %head_gate_hbm.1, bf16[1,128,512]{2,1,0:T(8,128)(2,1)} %q_hbm.1, bf16[1,128,128]{2,1,0:T(8,128)(2,1)} %k_hbm.1, bf16[1,128,128]{2,1,0:T(8,128)(2,1)} %v_hbm.1, bf16[1,128,512]{2,1,0:T(8,128)(2,1)} %grad_hbm.1, ...), custom_call_target="tpu_custom_call" | custom-call | tf_op jit(solution)/shard_map/front/pallas_call | solution.py:119
  4.2 10.5 %all-to-all-start = ((bf16[32,136,128]{2,1,0:T(8,128)(2,1)}), bf16[32,136,128]{2,1,0:T(8,128)(2,1)S(1)}, u32[]{:S(2)}, u32[]{:S(2)}) async-start(bf16[32,136,128]{2,1,0:T(8,128)(2,1)} %get-tuple-element.17), calls=%async_computation | async-start | bytes 2228224 | tf_op jit(solution)/shard_map/all_to_all | solution.py:227
  15.3 2.2 %collective-permute-start.1 = (f32[8,128]{1,0:T(8,128)S(1)}, f32[8,128]{1,0:T(8,128)S(1)}, u32[]{:S(2)}, u32[]{:S(2)}) collective-permute-start(f32[8,128]{1,0:T(8,128)S(1)} %broadcast_in_dim.9.own_gate_ref.gate_ref), channel_id=1, source_target_pairs={{0,8},{8,0},{1,9},{9,1},{2,10},{10,2},{3,11},{11,3},{4,12},{12,4},... | collective-permute-start | bytes 12296 | tf_op jit(solution)/shard_map/ppermute | solution.py:230
  17.6 3.3 %collective-permute-start = (f32[8,128]{1,0:T(8,128)S(1)}, f32[8,128]{1,0:T(8,128)S(1)}, u32[]{:S(2)}, u32[]{:S(2)}) collective-permute-start(f32[8,128]{1,0:T(8,128)S(1)} %broadcast_in_dim.9.own_gate_ref.gate_ref), channel_id=1, source_target_pairs={{0,64},{64,0},{1,65},{65,1},{2,66},{66,2},{3,67},{67,3},{4,68},{68... | collective-permute-start | bytes 12296 | tf_op jit(solution)/shard_map/ppermute | solution.py:231
  20.9 0.0 collective-permute-done.1.core_gate_ref
  20.9 2.0 %collective-permute-start.2 = (f32[8,128]{1,0:T(8,128)S(1)}, f32[8,128]{1,0:T(8,128)S(1)}, u32[]{:S(2)}, u32[]{:S(2)}) collective-permute-start(f32[8,128]{1,0:T(8,128)S(1)} %collective-permute-done.1.core_gate_ref), channel_id=1, source_target_pairs={{0,64},{64,0},{1,65},{65,1},{2,66},{66,2},{3,67},{67,3},{4,68},{68... | collective-permute-start | bytes 12296 | tf_op jit(solution)/shard_map/ppermute | solution.py:232
  22.9 6.0 %collective-permute-done.y_gate_ref = f32[8,128]{1,0:T(8,128)S(1)} collective-permute-done((f32[8,128]{1,0:T(8,128)S(1)}, f32[8,128]{1,0:T(8,128)S(1)}, u32[]{:S(2)}, u32[]{:S(2)}) %collective-permute-start) | collective-permute-done | bytes 4128 | tf_op jit(solution)/shard_map/ppermute | solution.py:231
  28.9 0.1 collective-permute-done.2.both_gate_ref
  29.0 2.7 %all-to-all-done.parts_ref = bf16[32,136,128]{2,1,0:T(8,128)(2,1)S(1)} async-done(((bf16[32,136,128]{2,1,0:T(8,128)(2,1)}), bf16[32,136,128]{2,1,0:T(8,128)(2,1)S(1)}, u32[]{:S(2)}, u32[]{:S(2)}) %all-to-all-start) | async-done | bytes 1114144 | tf_op jit(solution)/shard_map/all_to_all | solution.py:227
  31.7 0.2 terms.1
  31.9 0.0 copy-start
  31.9 1.3 %collective-permute-start.3 = (bf16[128,128]{1,0:T(8,128)(2,1)S(1)}, bf16[128,128]{1,0:T(8,128)(2,1)S(1)}, u32[]{:S(2)}, u32[]{:S(2)}) collective-permute-start(bf16[128,128]{1,0:T(8,128)(2,1)S(1)} %get-tuple-element.20), channel_id=1, source_target_pairs={{384,0},{385,1},{386,2},{387,3},{388,4},{389,5},{390,6},{391,7},{3... | collective-permute-start | bytes 98312 | tf_op jit(solution)/shard_map/ppermute | solution.py:245
  33.2 1.3 %collective-permute-start.4 = (bf16[128,128]{1,0:T(8,128)(2,1)S(1)}, bf16[128,128]{1,0:T(8,128)(2,1)S(1)}, u32[]{:S(2)}, u32[]{:S(2)}) collective-permute-start(bf16[128,128]{1,0:T(8,128)(2,1)S(1)} %get-tuple-element.20), channel_id=1, source_target_pairs={{256,0},{384,128},{257,1},{385,129},{258,2},{386,130},{259,3},{387... | collective-permute-start | bytes 98312 | tf_op jit(solution)/shard_map/ppermute | solution.py:245
  34.5 1.3 %collective-permute-start.5 = (bf16[128,128]{1,0:T(8,128)(2,1)S(1)}, bf16[128,128]{1,0:T(8,128)(2,1)S(1)}, u32[]{:S(2)}, u32[]{:S(2)}) collective-permute-start(bf16[128,128]{1,0:T(8,128)(2,1)S(1)} %get-tuple-element.20), channel_id=1, source_target_pairs={{128,0},{256,128},{384,256},{129,1},{257,129},{385,257},{130,2},{2... | collective-permute-start | bytes 98312 | tf_op jit(solution)/shard_map/ppermute | solution.py:245
  35.8 2.9 %collective-permute-done.3.far_1 = bf16[128,128]{1,0:T(8,128)(2,1)S(1)} collective-permute-done((bf16[128,128]{1,0:T(8,128)(2,1)S(1)}, bf16[128,128]{1,0:T(8,128)(2,1)S(1)}, u32[]{:S(2)}, u32[]{:S(2)}) %collective-permute-start.3) | collective-permute-done | bytes 32800 | tf_op jit(solution)/shard_map/ppermute | solution.py:245
  38.7 3.2 %collective-permute-done.4.far_2 = bf16[128,128]{1,0:T(8,128)(2,1)S(1)} collective-permute-done((bf16[128,128]{1,0:T(8,128)(2,1)S(1)}, bf16[128,128]{1,0:T(8,128)(2,1)S(1)}, u32[]{:S(2)}, u32[]{:S(2)}) %collective-permute-start.4) | collective-permute-done | bytes 32800 | tf_op jit(solution)/shard_map/ppermute | solution.py:245
  41.9 0.0 collective-permute-done.5.far_3
  41.9 1.3 %collective-permute-start.6 = (bf16[2,128,128]{2,1,0:T(8,128)(2,1)S(1)}, bf16[2,128,128]{2,1,0:T(8,128)(2,1)S(1)}, u32[]{:S(2)}, u32[]{:S(2)}) collective-permute-start(bf16[2,128,128]{2,1,0:T(8,128)(2,1)S(1)} %get-tuple-element.22), channel_id=1, source_target_pairs={{48,0},{32,16},{49,1},{33,17},{50,2},{34,18},{51,3},{35,19},{52,4}... | collective-permute-start | bytes 196616 | tf_op jit(solution)/shard_map/ppermute | solution.py:259
  43.2 1.3 %collective-permute-start.7 = (bf16[2,128,128]{2,1,0:T(8,128)(2,1)S(1)}, bf16[2,128,128]{2,1,0:T(8,128)(2,1)S(1)}, u32[]{:S(2)}, u32[]{:S(2)}) collective-permute-start(bf16[2,128,128]{2,1,0:T(8,128)(2,1)S(1)} %get-tuple-element.22), channel_id=1, source_target_pairs={{32,0},{48,16},{33,1},{49,17},{34,2},{50,18},{35,3},{51,19},{36,4}... | collective-permute-start | bytes 196616 | tf_op jit(solution)/shard_map/ppermute | solution.py:260
  44.5 3.9 %collective-permute-start.8 = (bf16[2,128,128]{2,1,0:T(8,128)(2,1)S(1)}, bf16[2,128,128]{2,1,0:T(8,128)(2,1)S(1)}, u32[]{:S(2)}, u32[]{:S(2)}) collective-permute-start(bf16[2,128,128]{2,1,0:T(8,128)(2,1)S(1)} %get-tuple-element.23), channel_id=1, source_target_pairs={{0,16},{16,0},{1,17},{17,1},{2,18},{18,2},{3,19},{19,3},{4,20},{20... | collective-permute-start | bytes 196616 | tf_op jit(solution)/shard_map/ppermute | solution.py:261
  48.4 4.6 %collective-permute-start.10 = (bf16[2,128,128]{2,1,0:T(8,128)(2,1)S(1)}, bf16[2,128,128]{2,1,0:T(8,128)(2,1)S(1)}, u32[]{:S(2)}, u32[]{:S(2)}) collective-permute-start(bf16[2,128,128]{2,1,0:T(8,128)(2,1)S(1)} %get-tuple-element.23), channel_id=1, source_target_pairs={{0,48},{1,49},{2,50},{3,51},{4,52},{5,53},{6,54},{7,55},{8,56},{9,... | collective-permute-start | bytes 196616 | tf_op jit(solution)/shard_map/ppermute | solution.py:269
  53.1 0.7 %collective-permute-start.9 = (bf16[2,128,128]{2,1,0:T(8,128)(2,1)S(1)}, bf16[2,128,128]{2,1,0:T(8,128)(2,1)S(1)}, u32[]{:S(2)}, u32[]{:S(2)}) collective-permute-start(bf16[2,128,128]{2,1,0:T(8,128)(2,1)S(1)} %get-tuple-element.25), channel_id=1, source_target_pairs={{48,32},{16,48},{49,33},{17,49},{50,34},{18,50},{51,35},{19,51},{5... | collective-permute-start | bytes 196616 | tf_op jit(solution)/shard_map/ppermute | solution.py:268
  53.7 0.0 collective-permute-done.6.step_1
  53.7 0.0 collective-permute-done.7.step_2
  53.8 0.0 collective-permute-done.8.step_3
  53.8 0.1 pass_on.1
  53.8 0.7 %collective-permute-start.11 = (bf16[2,128,128]{2,1,0:T(8,128)(2,1)S(1)}, bf16[2,128,128]{2,1,0:T(8,128)(2,1)S(1)}, u32[]{:S(2)}, u32[]{:S(2)}) collective-permute-start(bf16[2,128,128]{2,1,0:T(8,128)(2,1)S(1)} %get-tuple-element.26), channel_id=1, source_target_pairs={{16,32},{32,48},{17,33},{33,49},{18,34},{34,50},{19,35},{35,51},{2... | collective-permute-start | bytes 196616 | tf_op jit(solution)/shard_map/ppermute | solution.py:270
  54.5 0.0 collective-permute-done.9.step_5
  54.5 0.0 collective-permute-done.10.step_6
  54.5 0.1 sums.1
  54.6 10.6 %all_to_all.10.blocks_ref = bf16[4,128,128]{2,1,0:T(8,128)(2,1)S(1)} all-to-all(bf16[4,128,128]{2,1,0:T(8,128)(2,1)S(1)} %sums.1), channel_id=1, replica_groups=mesh['yh'=4,'yl'=2,'zh'=4,'core'=2,'zl'=2,'x'=4] {'core','yl'}, dimensions={0} | all-to-all | bytes 262144 | tf_op jit(solution)/shard_map/all_to_all | solution.py:274
  65.3 0.7 %join.1 = (bf16[1,128,512]{2,1,0:T(8,128)(2,1)}, f32[1,4]{1,0:T(1,128)}, f32[1]{0:T(128)}) custom-call(bf16[4,128,128]{2,1,0:T(8,128)(2,1)S(1)} %all_to_all.10.blocks_ref, f32[8,128]{1,0:T(8,128)S(1)} %get-tuple-element.27.share_ref, f32[8,128]{1,0:T(8,128)S(1)} %broadcast_in_dim.9.own_gate_ref.gate_ref, f32[1,128]{1,0:T(1,128)S(1)} %copy-done), custom_call_target="tpu_custom_call" | custom-call | tf_op jit(solution)/shard_map/join/pallas_call | solution.py:275
  (4 shorter events, 0.0 us)
Async XLA Ops:
  4.2 27.6 %all-to-all-start = ((bf16[32,136,128]{2,1,0:T(8,128)(2,1)}), bf16[32,136,128]{2,1,0:T(8,128)(2,1)S(1)}, u32[]{:S(2)}, u32[]{:S(2)}) async-start(bf16[32,136,128]{2,1,0:T(8,128)(2,1)} %get-tuple-element.17), calls=%async_computation | async-start | bytes 2228224 | tf_op jit(solution)/shard_map/all_to_all | solution.py:227
  15.3 5.6 %collective-permute-start.1 = (f32[8,128]{1,0:T(8,128)S(1)}, f32[8,128]{1,0:T(8,128)S(1)}, u32[]{:S(2)}, u32[]{:S(2)}) collective-permute-start(f32[8,128]{1,0:T(8,128)S(1)} %broadcast_in_dim.9.own_gate_ref.gate_ref), channel_id=1, source_target_pairs={{0,8},{8,0},{1,9},{9,1},{2,10},{10,2},{3,11},{11,3},{4,12},{12,4},... | collective-permute-start | bytes 12296 | tf_op jit(solution)/shard_map/ppermute | solution.py:230
  17.6 11.3 %collective-permute-start = (f32[8,128]{1,0:T(8,128)S(1)}, f32[8,128]{1,0:T(8,128)S(1)}, u32[]{:S(2)}, u32[]{:S(2)}) collective-permute-start(f32[8,128]{1,0:T(8,128)S(1)} %broadcast_in_dim.9.own_gate_ref.gate_ref), channel_id=1, source_target_pairs={{0,64},{64,0},{1,65},{65,1},{2,66},{66,2},{3,67},{67,3},{4,68},{68... | collective-permute-start | bytes 12296 | tf_op jit(solution)/shard_map/ppermute | solution.py:231
  20.9 8.1 %collective-permute-start.2 = (f32[8,128]{1,0:T(8,128)S(1)}, f32[8,128]{1,0:T(8,128)S(1)}, u32[]{:S(2)}, u32[]{:S(2)}) collective-permute-start(f32[8,128]{1,0:T(8,128)S(1)} %collective-permute-done.1.core_gate_ref), channel_id=1, source_target_pairs={{0,64},{64,0},{1,65},{65,1},{2,66},{66,2},{3,67},{67,3},{4,68},{68... | collective-permute-start | bytes 12296 | tf_op jit(solution)/shard_map/ppermute | solution.py:232
  31.9 33.4 %copy-start = (f32[1,128]{1,0:T(1,128)S(1)}, f32[1,128]{1,0:T(1,128)}, u32[]{:S(2)}) copy-start(f32[1,128]{1,0:T(1,128)} %get-tuple-element.28.head_sum_ref) | copy-start | bytes 1540
  31.9 6.8 %collective-permute-start.3 = (bf16[128,128]{1,0:T(8,128)(2,1)S(1)}, bf16[128,128]{1,0:T(8,128)(2,1)S(1)}, u32[]{:S(2)}, u32[]{:S(2)}) collective-permute-start(bf16[128,128]{1,0:T(8,128)(2,1)S(1)} %get-tuple-element.20), channel_id=1, source_target_pairs={{384,0},{385,1},{386,2},{387,3},{388,4},{389,5},{390,6},{391,7},{3... | collective-permute-start | bytes 98312 | tf_op jit(solution)/shard_map/ppermute | solution.py:245
  33.2 8.7 %collective-permute-start.4 = (bf16[128,128]{1,0:T(8,128)(2,1)S(1)}, bf16[128,128]{1,0:T(8,128)(2,1)S(1)}, u32[]{:S(2)}, u32[]{:S(2)}) collective-permute-start(bf16[128,128]{1,0:T(8,128)(2,1)S(1)} %get-tuple-element.20), channel_id=1, source_target_pairs={{256,0},{384,128},{257,1},{385,129},{258,2},{386,130},{259,3},{387... | collective-permute-start | bytes 98312 | tf_op jit(solution)/shard_map/ppermute | solution.py:245
  34.5 7.4 %collective-permute-start.5 = (bf16[128,128]{1,0:T(8,128)(2,1)S(1)}, bf16[128,128]{1,0:T(8,128)(2,1)S(1)}, u32[]{:S(2)}, u32[]{:S(2)}) collective-permute-start(bf16[128,128]{1,0:T(8,128)(2,1)S(1)} %get-tuple-element.20), channel_id=1, source_target_pairs={{128,0},{256,128},{384,256},{129,1},{257,129},{385,257},{130,2},{2... | collective-permute-start | bytes 98312 | tf_op jit(solution)/shard_map/ppermute | solution.py:245
  41.9 11.8 %collective-permute-start.6 = (bf16[2,128,128]{2,1,0:T(8,128)(2,1)S(1)}, bf16[2,128,128]{2,1,0:T(8,128)(2,1)S(1)}, u32[]{:S(2)}, u32[]{:S(2)}) collective-permute-start(bf16[2,128,128]{2,1,0:T(8,128)(2,1)S(1)} %get-tuple-element.22), channel_id=1, source_target_pairs={{48,0},{32,16},{49,1},{33,17},{50,2},{34,18},{51,3},{35,19},{52,4}... | collective-permute-start | bytes 196616 | tf_op jit(solution)/shard_map/ppermute | solution.py:259
  43.2 10.5 %collective-permute-start.7 = (bf16[2,128,128]{2,1,0:T(8,128)(2,1)S(1)}, bf16[2,128,128]{2,1,0:T(8,128)(2,1)S(1)}, u32[]{:S(2)}, u32[]{:S(2)}) collective-permute-start(bf16[2,128,128]{2,1,0:T(8,128)(2,1)S(1)} %get-tuple-element.22), channel_id=1, source_target_pairs={{32,0},{48,16},{33,1},{49,17},{34,2},{50,18},{35,3},{51,19},{36,4}... | collective-permute-start | bytes 196616 | tf_op jit(solution)/shard_map/ppermute | solution.py:260
  44.5 9.2 %collective-permute-start.8 = (bf16[2,128,128]{2,1,0:T(8,128)(2,1)S(1)}, bf16[2,128,128]{2,1,0:T(8,128)(2,1)S(1)}, u32[]{:S(2)}, u32[]{:S(2)}) collective-permute-start(bf16[2,128,128]{2,1,0:T(8,128)(2,1)S(1)} %get-tuple-element.23), channel_id=1, source_target_pairs={{0,16},{16,0},{1,17},{17,1},{2,18},{18,2},{3,19},{19,3},{4,20},{20... | collective-permute-start | bytes 196616 | tf_op jit(solution)/shard_map/ppermute | solution.py:261
  48.4 6.1 %collective-permute-start.10 = (bf16[2,128,128]{2,1,0:T(8,128)(2,1)S(1)}, bf16[2,128,128]{2,1,0:T(8,128)(2,1)S(1)}, u32[]{:S(2)}, u32[]{:S(2)}) collective-permute-start(bf16[2,128,128]{2,1,0:T(8,128)(2,1)S(1)} %get-tuple-element.23), channel_id=1, source_target_pairs={{0,48},{1,49},{2,50},{3,51},{4,52},{5,53},{6,54},{7,55},{8,56},{9,... | collective-permute-start | bytes 196616 | tf_op jit(solution)/shard_map/ppermute | solution.py:269
  53.1 1.4 %collective-permute-start.9 = (bf16[2,128,128]{2,1,0:T(8,128)(2,1)S(1)}, bf16[2,128,128]{2,1,0:T(8,128)(2,1)S(1)}, u32[]{:S(2)}, u32[]{:S(2)}) collective-permute-start(bf16[2,128,128]{2,1,0:T(8,128)(2,1)S(1)} %get-tuple-element.25), channel_id=1, source_target_pairs={{48,32},{16,48},{49,33},{17,49},{50,34},{18,50},{51,35},{19,51},{5... | collective-permute-start | bytes 196616 | tf_op jit(solution)/shard_map/ppermute | solution.py:268
  53.8 0.7 %collective-permute-start.11 = (bf16[2,128,128]{2,1,0:T(8,128)(2,1)S(1)}, bf16[2,128,128]{2,1,0:T(8,128)(2,1)S(1)}, u32[]{:S(2)}, u32[]{:S(2)}) collective-permute-start(bf16[2,128,128]{2,1,0:T(8,128)(2,1)S(1)} %get-tuple-element.26), channel_id=1, source_target_pairs={{16,32},{32,48},{17,33},{33,49},{18,34},{34,50},{19,35},{35,51},{2... | collective-permute-start | bytes 196616 | tf_op jit(solution)/shard_map/ppermute | solution.py:270

commit v5 on v4

--- a/solution.py
+++ b/solution.py
@@ -140,7 +140,12 @@
     )(order, head_gate, q, k, v, grad, kw, vw)
 
 
-def terms_kernel(parts_ref, own_gate_ref, y_gate_ref, core_gate_ref, both_gate_ref, terms_ref, totals_ref, share_ref):
+def pair_kernel(own_ref, core_ref, pair_ref):
+    row = lax.broadcasted_iota(jnp.int32, own_ref.shape, 0)
+    pair_ref[...] = jnp.where(row < EXTRA // 2, own_ref[...], core_ref[...])
+
+
+def terms_kernel(parts_ref, gates_ref, y_gates_ref, terms_ref, totals_ref, share_ref):
     own = lax.axis_index("core") * 2 + lax.axis_index("yl")
     total = jnp.zeros((BLOCK, SEQ), F32)
     share = jnp.zeros((EXTRA, SEQ), F32)
@@ -151,14 +156,14 @@
         apart = own ^ n
         gate = jnp.where(
             apart == 0,
-            own_gate_ref[...],
+            gates_ref[:1],
             jnp.where(
                 apart == 1,
-                y_gate_ref[...],
-                jnp.where(apart == 2, core_gate_ref[...], both_gate_ref[...]),
+                y_gates_ref[:1],
+                jnp.where(apart == 2, gates_ref[EXTRA // 2:][:1], y_gates_ref[EXTRA // 2:][:1]),
             ),
         )
-        scaled = term[:BLOCK] * gate[:1]
+        scaled = term[:BLOCK] * gate
         terms_ref[n] = scaled
         total += scaled
         share += jnp.where(own == n, term[BLOCK:], 0.0)
@@ -228,8 +233,10 @@
     gate = jnp.broadcast_to(layer_gate[:, None], (EXTRA, SEQ))
     swap = ((0, 1), (1, 0))
     core_gate = lax.ppermute(gate, "core", swap)
-    y_gate = lax.ppermute(gate, "yl", swap)
-    both_gate = lax.ppermute(core_gate, "yl", swap)
+    gates = small(pair_kernel, "gate_pair", jax.ShapeDtypeStruct((EXTRA, SEQ), F32))(
+        gate, core_gate
+    )
+    y_gates = lax.ppermute(gates, "yl", swap)
     vmem = pl.BlockSpec(memory_space=pltpu.VMEM)
     terms, totals, share = small(
         terms_kernel,
@@ -240,7 +247,7 @@
             jax.ShapeDtypeStruct((EXTRA, SEQ), F32),
         ),
         (vmem, vmem, vmem),
-    )(parts, gate, y_gate, core_gate, both_gate)
+    )(parts, gates, y_gates)
     totals = [
         lax.ppermute(totals, "yh", [(f, f - step) for f in range(step, FAR)]) for step in (3, 2, 1)
     ]

time: 66.5 us -> 66.4 us (level)
  starting transfers between devices: 34.3 us -> 32.3 us
  waiting for transfers between devices: 14.9 us -> 16.9 us
    ppermute x2 -> x1, starting transfers between devices: 5.28 us -> 3.29 us  [body(): y_gates = lax.ppermute(gates, 'yl', swap)]
    ppermute x2 -> x1, waiting for transfers between devices: 6.13 us -> 7.24 us  [body(): y_gates = lax.ppermute(gates, 'yl', swap)]
    ppermute x1, waiting for transfers between devices: 0.01 us -> 0.8 us  [body(): core_gate = lax.ppermute(gate, 'core', swap)]
  transfers between devices with their start and end apart: 13 -> 12, of which waited for: 5 -> 5; matrix products, arithmetic and copies ran while one was open for 0% -> 0% of each run, Pallas kernels for 0% -> 0%
where the time goes in v5:
time: 66.4 us; the launch traced here: 65.9 us
  starting transfers between devices  32.3 us (49%)
  waiting for transfers between devices  16.9 us (25%)
  blocking collectives  10.6 us (16%)
  Pallas kernels  4.57 us (7%)
  between operations  1.46 us (2%)
    all_to_all x1, blocking collectives, body(): sums = lax.all_to_all(sums, NEAR_AXES, 0, 0)  10.6 us
    all_to_all x1, starting transfers between devices, body(): parts = lax.all_to_all(part, TENSOR_AXES + NEAR_AXES, 0, 0)  10.5 us
    ppermute x1, waiting for transfers between devices, body(): y_gates = lax.ppermute(gates, 'yl', swap)  7.24 us
    ppermute x3, waiting for transfers between devices, body(): lax.ppermute(totals, 'yh', [(f, f - step) for f in range(step, FAR)])  6.07 us
    ppermute x1, starting transfers between devices, body(): step_6 = lax.ppermute(first_later, 'zh', STEP_6)  4.62 us
    ppermute x1, starting transfers between devices, body(): step_3 = lax.ppermute(first_later, 'zh', STEP_3)  3.9 us
    ppermute x3, starting transfers between devices, body(): lax.ppermute(totals, 'yh', [(f, f - step) for f in range(step, FAR)])  3.88 us
    pallas_call x1, Pallas kernels, front(): pl.pallas_call(front_kernel, name='front', out_shape=(jax.ShapeDtypeStruc...  3.51 us
  transfers between devices with their start and end apart: 12, of which 5 were waited for; matrix products, arithmetic and copies ran while one was open for 0% of the time, Pallas kernels for 0%

profile of v5, /device:TPU:1, one launch (start us, length us, event | category | flops | bytes accessed | tf_op | source)
XLA Modules:
  0.0 65.9 jit_solution(18079700477527768517)
XLA Ops:
  0.6 3.5 %front.1 = (bf16[32,136,128]{2,1,0:T(8,128)(2,1)}, f32[1,128]{1,0:T(1,128)}) custom-call(s32[1,32]{1,0:T(1,128)} %order_hbm.1, f32[1,4]{1,0:T(1,128)} %head_gate_hbm.1, bf16[1,128,512]{2,1,0:T(8,128)(2,1)} %q_hbm.1, bf16[1,128,128]{2,1,0:T(8,128)(2,1)} %k_hbm.1, bf16[1,128,128]{2,1,0:T(8,128)(2,1)} %v_hbm.1, bf16[1,128,512]{2,1,0:T(8,128)(2,1)} %grad_hbm.1, ...), custom_call_target="tpu_custom_call" | custom-call | tf_op jit(solution)/shard_map/front/pallas_call | solution.py:119
  4.1 10.5 %all-to-all-start = ((bf16[32,136,128]{2,1,0:T(8,128)(2,1)}), bf16[32,136,128]{2,1,0:T(8,128)(2,1)S(1)}, u32[]{:S(2)}, u32[]{:S(2)}) async-start(bf16[32,136,128]{2,1,0:T(8,128)(2,1)} %get-tuple-element.17), calls=%async_computation | async-start | bytes 2228224 | tf_op jit(solution)/shard_map/all_to_all | solution.py:232
  15.3 2.2 %collective-permute-start = (f32[8,128]{1,0:T(8,128)S(1)}, f32[8,128]{1,0:T(8,128)S(1)}, u32[]{:S(2)}, u32[]{:S(2)}) collective-permute-start(f32[8,128]{1,0:T(8,128)S(1)} %broadcast_in_dim.9.own_ref.gate_ref), channel_id=1, source_target_pairs={{0,8},{8,0},{1,9},{9,1},{2,10},{10,2},{3,11},{11,3},{4,12},{12,4},... | collective-permute-start | bytes 12296 | tf_op jit(solution)/shard_map/ppermute | solution.py:235
  17.6 0.8 %collective-permute-done.core_ref = f32[8,128]{1,0:T(8,128)S(1)} collective-permute-done((f32[8,128]{1,0:T(8,128)S(1)}, f32[8,128]{1,0:T(8,128)S(1)}, u32[]{:S(2)}, u32[]{:S(2)}) %collective-permute-start) | collective-permute-done | bytes 4128 | tf_op jit(solution)/shard_map/ppermute | solution.py:235
  18.4 3.3 %collective-permute-start.1 = (f32[8,128]{1,0:T(8,128)S(1)}, f32[8,128]{1,0:T(8,128)S(1)}, u32[]{:S(2)}, u32[]{:S(2)}) collective-permute-start(f32[8,128]{1,0:T(8,128)S(1)} %gate_pair.1.gates_ref), channel_id=1, source_target_pairs={{0,64},{64,0},{1,65},{65,1},{2,66},{66,2},{3,67},{67,3},{4,68},{68... | collective-permute-start | bytes 12296 | tf_op jit(solution)/shard_map/ppermute | solution.py:239
  21.7 7.2 %collective-permute-done.1.y_gates_ref = f32[8,128]{1,0:T(8,128)S(1)} collective-permute-done((f32[8,128]{1,0:T(8,128)S(1)}, f32[8,128]{1,0:T(8,128)S(1)}, u32[]{:S(2)}, u32[]{:S(2)}) %collective-permute-start.1) | collective-permute-done | bytes 4128 | tf_op jit(solution)/shard_map/ppermute | solution.py:239
  28.9 2.8 %all-to-all-done.parts_ref = bf16[32,136,128]{2,1,0:T(8,128)(2,1)S(1)} async-done(((bf16[32,136,128]{2,1,0:T(8,128)(2,1)}), bf16[32,136,128]{2,1,0:T(8,128)(2,1)S(1)}, u32[]{:S(2)}, u32[]{:S(2)}) %all-to-all-start) | async-done | bytes 1114144 | tf_op jit(solution)/shard_map/all_to_all | solution.py:232
  31.7 0.2 terms.1
  31.9 0.0 copy-start
  31.9 1.3 %collective-permute-start.2 = (bf16[128,128]{1,0:T(8,128)(2,1)S(1)}, bf16[128,128]{1,0:T(8,128)(2,1)S(1)}, u32[]{:S(2)}, u32[]{:S(2)}) collective-permute-start(bf16[128,128]{1,0:T(8,128)(2,1)S(1)} %get-tuple-element.20), channel_id=1, source_target_pairs={{384,0},{385,1},{386,2},{387,3},{388,4},{389,5},{390,6},{391,7},{3... | collective-permute-start | bytes 98312 | tf_op jit(solution)/shard_map/ppermute | solution.py:252
  33.2 1.3 %collective-permute-start.3 = (bf16[128,128]{1,0:T(8,128)(2,1)S(1)}, bf16[128,128]{1,0:T(8,128)(2,1)S(1)}, u32[]{:S(2)}, u32[]{:S(2)}) collective-permute-start(bf16[128,128]{1,0:T(8,128)(2,1)S(1)} %get-tuple-element.20), channel_id=1, source_target_pairs={{256,0},{384,128},{257,1},{385,129},{258,2},{386,130},{259,3},{387... | collective-permute-start | bytes 98312 | tf_op jit(solution)/shard_map/ppermute | solution.py:252
  34.5 1.3 %collective-permute-start.4 = (bf16[128,128]{1,0:T(8,128)(2,1)S(1)}, bf16[128,128]{1,0:T(8,128)(2,1)S(1)}, u32[]{:S(2)}, u32[]{:S(2)}) collective-permute-start(bf16[128,128]{1,0:T(8,128)(2,1)S(1)} %get-tuple-element.20), channel_id=1, source_target_pairs={{128,0},{256,128},{384,256},{129,1},{257,129},{385,257},{130,2},{2... | collective-permute-start | bytes 98312 | tf_op jit(solution)/shard_map/ppermute | solution.py:252
  35.8 2.9 %collective-permute-done.2.far_1 = bf16[128,128]{1,0:T(8,128)(2,1)S(1)} collective-permute-done((bf16[128,128]{1,0:T(8,128)(2,1)S(1)}, bf16[128,128]{1,0:T(8,128)(2,1)S(1)}, u32[]{:S(2)}, u32[]{:S(2)}) %collective-permute-start.2) | collective-permute-done | bytes 32800 | tf_op jit(solution)/shard_map/ppermute | solution.py:252
  38.7 3.2 %collective-permute-done.3.far_2 = bf16[128,128]{1,0:T(8,128)(2,1)S(1)} collective-permute-done((bf16[128,128]{1,0:T(8,128)(2,1)S(1)}, bf16[128,128]{1,0:T(8,128)(2,1)S(1)}, u32[]{:S(2)}, u32[]{:S(2)}) %collective-permute-start.3) | collective-permute-done | bytes 32800 | tf_op jit(solution)/shard_map/ppermute | solution.py:252
  41.9 0.0 collective-permute-done.4.far_3
  41.9 1.3 %collective-permute-start.5 = (bf16[2,128,128]{2,1,0:T(8,128)(2,1)S(1)}, bf16[2,128,128]{2,1,0:T(8,128)(2,1)S(1)}, u32[]{:S(2)}, u32[]{:S(2)}) collective-permute-start(bf16[2,128,128]{2,1,0:T(8,128)(2,1)S(1)} %get-tuple-element.22), channel_id=1, source_target_pairs={{48,0},{32,16},{49,1},{33,17},{50,2},{34,18},{51,3},{35,19},{52,4}... | collective-permute-start | bytes 196616 | tf_op jit(solution)/shard_map/ppermute | solution.py:266
  43.2 1.3 %collective-permute-start.6 = (bf16[2,128,128]{2,1,0:T(8,128)(2,1)S(1)}, bf16[2,128,128]{2,1,0:T(8,128)(2,1)S(1)}, u32[]{:S(2)}, u32[]{:S(2)}) collective-permute-start(bf16[2,128,128]{2,1,0:T(8,128)(2,1)S(1)} %get-tuple-element.22), channel_id=1, source_target_pairs={{32,0},{48,16},{33,1},{49,17},{34,2},{50,18},{35,3},{51,19},{36,4}... | collective-permute-start | bytes 196616 | tf_op jit(solution)/shard_map/ppermute | solution.py:267
  44.5 3.9 %collective-permute-start.7 = (bf16[2,128,128]{2,1,0:T(8,128)(2,1)S(1)}, bf16[2,128,128]{2,1,0:T(8,128)(2,1)S(1)}, u32[]{:S(2)}, u32[]{:S(2)}) collective-permute-start(bf16[2,128,128]{2,1,0:T(8,128)(2,1)S(1)} %get-tuple-element.23), channel_id=1, source_target_pairs={{0,16},{16,0},{1,17},{17,1},{2,18},{18,2},{3,19},{19,3},{4,20},{20... | collective-permute-start | bytes 196616 | tf_op jit(solution)/shard_map/ppermute | solution.py:268
  48.4 4.6 %collective-permute-start.9 = (bf16[2,128,128]{2,1,0:T(8,128)(2,1)S(1)}, bf16[2,128,128]{2,1,0:T(8,128)(2,1)S(1)}, u32[]{:S(2)}, u32[]{:S(2)}) collective-permute-start(bf16[2,128,128]{2,1,0:T(8,128)(2,1)S(1)} %get-tuple-element.23), channel_id=1, source_target_pairs={{0,48},{1,49},{2,50},{3,51},{4,52},{5,53},{6,54},{7,55},{8,56},{9,... | collective-permute-start | bytes 196616 | tf_op jit(solution)/shard_map/ppermute | solution.py:276
  53.1 0.7 %collective-permute-start.8 = (bf16[2,128,128]{2,1,0:T(8,128)(2,1)S(1)}, bf16[2,128,128]{2,1,0:T(8,128)(2,1)S(1)}, u32[]{:S(2)}, u32[]{:S(2)}) collective-permute-start(bf16[2,128,128]{2,1,0:T(8,128)(2,1)S(1)} %get-tuple-element.25), channel_id=1, source_target_pairs={{48,32},{16,48},{49,33},{17,49},{50,34},{18,50},{51,35},{19,51},{5... | collective-permute-start | bytes 196616 | tf_op jit(solution)/shard_map/ppermute | solution.py:275
  53.7 0.0 collective-permute-done.5.step_1
  53.7 0.0 collective-permute-done.6.step_2
  53.7 0.0 collective-permute-done.7.step_3
  53.8 0.1 pass_on.1
  53.8 0.7 %collective-permute-start.10 = (bf16[2,128,128]{2,1,0:T(8,128)(2,1)S(1)}, bf16[2,128,128]{2,1,0:T(8,128)(2,1)S(1)}, u32[]{:S(2)}, u32[]{:S(2)}) collective-permute-start(bf16[2,128,128]{2,1,0:T(8,128)(2,1)S(1)} %get-tuple-element.26), channel_id=1, source_target_pairs={{16,32},{32,48},{17,33},{33,49},{18,34},{34,50},{19,35},{35,51},{2... | collective-permute-start | bytes 196616 | tf_op jit(solution)/shard_map/ppermute | solution.py:277
  54.5 0.0 collective-permute-done.8.step_5
  54.5 0.0 collective-permute-done.9.step_6
  54.5 0.0 collective-permute-done.10.step_4
  54.5 0.1 sums.1
  54.6 10.6 %all_to_all.10.blocks_ref = bf16[4,128,128]{2,1,0:T(8,128)(2,1)S(1)} all-to-all(bf16[4,128,128]{2,1,0:T(8,128)(2,1)S(1)} %sums.1), channel_id=1, replica_groups=mesh['yh'=4,'yl'=2,'zh'=4,'core'=2,'zl'=2,'x'=4] {'core','yl'}, dimensions={0} | all-to-all | bytes 262144 | tf_op jit(solution)/shard_map/all_to_all | solution.py:281
  65.2 0.0 copy-done
  65.2 0.7 %join.1 = (bf16[1,128,512]{2,1,0:T(8,128)(2,1)}, f32[1,4]{1,0:T(1,128)}, f32[1]{0:T(128)}) custom-call(bf16[4,128,128]{2,1,0:T(8,128)(2,1)S(1)} %all_to_all.10.blocks_ref, f32[8,128]{1,0:T(8,128)S(1)} %get-tuple-element.27.share_ref, f32[8,128]{1,0:T(8,128)S(1)} %broadcast_in_dim.9.own_ref.gate_ref, f32[1,128]{1,0:T(1,128)S(1)} %copy-done), custom_call_target="tpu_custom_call" | custom-call | tf_op jit(solution)/shard_map/join/pallas_call | solution.py:282
  (3 shorter events, 0.0 us)
Async XLA Ops:
  4.1 27.6 %all-to-all-start = ((bf16[32,136,128]{2,1,0:T(8,128)(2,1)}), bf16[32,136,128]{2,1,0:T(8,128)(2,1)S(1)}, u32[]{:S(2)}, u32[]{:S(2)}) async-start(bf16[32,136,128]{2,1,0:T(8,128)(2,1)} %get-tuple-element.17), calls=%async_computation | async-start | bytes 2228224 | tf_op jit(solution)/shard_map/all_to_all | solution.py:232
  15.3 3.1 %collective-permute-start = (f32[8,128]{1,0:T(8,128)S(1)}, f32[8,128]{1,0:T(8,128)S(1)}, u32[]{:S(2)}, u32[]{:S(2)}) collective-permute-start(f32[8,128]{1,0:T(8,128)S(1)} %broadcast_in_dim.9.own_ref.gate_ref), channel_id=1, source_target_pairs={{0,8},{8,0},{1,9},{9,1},{2,10},{10,2},{3,11},{11,3},{4,12},{12,4},... | collective-permute-start | bytes 12296 | tf_op jit(solution)/shard_map/ppermute | solution.py:235
  18.4 10.5 %collective-permute-start.1 = (f32[8,128]{1,0:T(8,128)S(1)}, f32[8,128]{1,0:T(8,128)S(1)}, u32[]{:S(2)}, u32[]{:S(2)}) collective-permute-start(f32[8,128]{1,0:T(8,128)S(1)} %gate_pair.1.gates_ref), channel_id=1, source_target_pairs={{0,64},{64,0},{1,65},{65,1},{2,66},{66,2},{3,67},{67,3},{4,68},{68... | collective-permute-start | bytes 12296 | tf_op jit(solution)/shard_map/ppermute | solution.py:239
  31.9 33.3 %copy-start = (f32[1,128]{1,0:T(1,128)S(1)}, f32[1,128]{1,0:T(1,128)}, u32[]{:S(2)}) copy-start(f32[1,128]{1,0:T(1,128)} %get-tuple-element.28.head_sum_ref) | copy-start | bytes 1540
  31.9 6.8 %collective-permute-start.2 = (bf16[128,128]{1,0:T(8,128)(2,1)S(1)}, bf16[128,128]{1,0:T(8,128)(2,1)S(1)}, u32[]{:S(2)}, u32[]{:S(2)}) collective-permute-start(bf16[128,128]{1,0:T(8,128)(2,1)S(1)} %get-tuple-element.20), channel_id=1, source_target_pairs={{384,0},{385,1},{386,2},{387,3},{388,4},{389,5},{390,6},{391,7},{3... | collective-permute-start | bytes 98312 | tf_op jit(solution)/shard_map/ppermute | solution.py:252
  33.2 8.7 %collective-permute-start.3 = (bf16[128,128]{1,0:T(8,128)(2,1)S(1)}, bf16[128,128]{1,0:T(8,128)(2,1)S(1)}, u32[]{:S(2)}, u32[]{:S(2)}) collective-permute-start(bf16[128,128]{1,0:T(8,128)(2,1)S(1)} %get-tuple-element.20), channel_id=1, source_target_pairs={{256,0},{384,128},{257,1},{385,129},{258,2},{386,130},{259,3},{387... | collective-permute-start | bytes 98312 | tf_op jit(solution)/shard_map/ppermute | solution.py:252
  34.5 7.4 %collective-permute-start.4 = (bf16[128,128]{1,0:T(8,128)(2,1)S(1)}, bf16[128,128]{1,0:T(8,128)(2,1)S(1)}, u32[]{:S(2)}, u32[]{:S(2)}) collective-permute-start(bf16[128,128]{1,0:T(8,128)(2,1)S(1)} %get-tuple-element.20), channel_id=1, source_target_pairs={{128,0},{256,128},{384,256},{129,1},{257,129},{385,257},{130,2},{2... | collective-permute-start | bytes 98312 | tf_op jit(solution)/shard_map/ppermute | solution.py:252
  41.9 11.8 %collective-permute-start.5 = (bf16[2,128,128]{2,1,0:T(8,128)(2,1)S(1)}, bf16[2,128,128]{2,1,0:T(8,128)(2,1)S(1)}, u32[]{:S(2)}, u32[]{:S(2)}) collective-permute-start(bf16[2,128,128]{2,1,0:T(8,128)(2,1)S(1)} %get-tuple-element.22), channel_id=1, source_target_pairs={{48,0},{32,16},{49,1},{33,17},{50,2},{34,18},{51,3},{35,19},{52,4}... | collective-permute-start | bytes 196616 | tf_op jit(solution)/shard_map/ppermute | solution.py:266
  43.2 10.5 %collective-permute-start.6 = (bf16[2,128,128]{2,1,0:T(8,128)(2,1)S(1)}, bf16[2,128,128]{2,1,0:T(8,128)(2,1)S(1)}, u32[]{:S(2)}, u32[]{:S(2)}) collective-permute-start(bf16[2,128,128]{2,1,0:T(8,128)(2,1)S(1)} %get-tuple-element.22), channel_id=1, source_target_pairs={{32,0},{48,16},{33,1},{49,17},{34,2},{50,18},{35,3},{51,19},{36,4}... | collective-permute-start | bytes 196616 | tf_op jit(solution)/shard_map/ppermute | solution.py:267
  44.5 9.2 %collective-permute-start.7 = (bf16[2,128,128]{2,1,0:T(8,128)(2,1)S(1)}, bf16[2,128,128]{2,1,0:T(8,128)(2,1)S(1)}, u32[]{:S(2)}, u32[]{:S(2)}) collective-permute-start(bf16[2,128,128]{2,1,0:T(8,128)(2,1)S(1)} %get-tuple-element.23), channel_id=1, source_target_pairs={{0,16},{16,0},{1,17},{17,1},{2,18},{18,2},{3,19},{19,3},{4,20},{20... | collective-permute-start | bytes 196616 | tf_op jit(solution)/shard_map/ppermute | solution.py:268
  48.4 6.1 %collective-permute-start.9 = (bf16[2,128,128]{2,1,0:T(8,128)(2,1)S(1)}, bf16[2,128,128]{2,1,0:T(8,128)(2,1)S(1)}, u32[]{:S(2)}, u32[]{:S(2)}) collective-permute-start(bf16[2,128,128]{2,1,0:T(8,128)(2,1)S(1)} %get-tuple-element.23), channel_id=1, source_target_pairs={{0,48},{1,49},{2,50},{3,51},{4,52},{5,53},{6,54},{7,55},{8,56},{9,... | collective-permute-start | bytes 196616 | tf_op jit(solution)/shard_map/ppermute | solution.py:276
  53.1 1.4 %collective-permute-start.8 = (bf16[2,128,128]{2,1,0:T(8,128)(2,1)S(1)}, bf16[2,128,128]{2,1,0:T(8,128)(2,1)S(1)}, u32[]{:S(2)}, u32[]{:S(2)}) collective-permute-start(bf16[2,128,128]{2,1,0:T(8,128)(2,1)S(1)} %get-tuple-element.25), channel_id=1, source_target_pairs={{48,32},{16,48},{49,33},{17,49},{50,34},{18,50},{51,35},{19,51},{5... | collective-permute-start | bytes 196616 | tf_op jit(solution)/shard_map/ppermute | solution.py:275
  53.8 0.7 %collective-permute-start.10 = (bf16[2,128,128]{2,1,0:T(8,128)(2,1)S(1)}, bf16[2,128,128]{2,1,0:T(8,128)(2,1)S(1)}, u32[]{:S(2)}, u32[]{:S(2)}) collective-permute-start(bf16[2,128,128]{2,1,0:T(8,128)(2,1)S(1)} %get-tuple-element.26), channel_id=1, source_target_pairs={{16,32},{32,48},{17,33},{33,49},{18,34},{34,50},{19,35},{35,51},{2... | collective-permute-start | bytes 196616 | tf_op jit(solution)/shard_map/ppermute | solution.py:277

commit v6 on v5

--- a/solution.py
+++ b/solution.py
@@ -136,8 +136,11 @@
             pltpu.VMEM(vw.shape, BF16),
             pltpu.SemaphoreType.DMA((8,)),
         ],
-        compiler_params=pltpu.CompilerParams(vmem_limit_bytes=58 * MIB),
-    )(order, head_gate, q, k, v, grad, kw, vw)
+        compiler_params=pltpu.CompilerParams(vmem_limit_bytes=24 * MIB),
+    )(*[
+        pltpu.with_memory_space_constraint(operand, pltpu.HBM)
+        for operand in (order, head_gate, q, k, v, grad, kw, vw)
+    ])
 
 
 def pair_kernel(own_ref, core_ref, pair_ref):

time: 66.4 us -> 66.4 us (level)
  no operation moved by 1% of the time
where the time goes in v6:
time: 66.4 us; the launch traced here: 65.9 us
  starting transfers between devices  32.3 us (49%)
  waiting for transfers between devices  16.9 us (25%)
  blocking collectives  10.6 us (16%)
  Pallas kernels  4.59 us (7%)
  between operations  1.46 us (2%)
    all_to_all x1, blocking collectives, body(): sums = lax.all_to_all(sums, NEAR_AXES, 0, 0)  10.6 us
    all_to_all x1, starting transfers between devices, body(): parts = lax.all_to_all(part, TENSOR_AXES + NEAR_AXES, 0, 0)  10.5 us
    ppermute x1, waiting for transfers between devices, body(): y_gates = lax.ppermute(gates, 'yl', swap)  7.24 us
    ppermute x3, waiting for transfers between devices, body(): lax.ppermute(totals, 'yh', [(f, f - step) for f in range(step, FAR)])  6.07 us
    ppermute x1, starting transfers between devices, body(): step_6 = lax.ppermute(first_later, 'zh', STEP_6)  4.61 us
    ppermute x1, starting transfers between devices, body(): step_3 = lax.ppermute(first_later, 'zh', STEP_3)  3.91 us
    ppermute x3, starting transfers between devices, body(): lax.ppermute(totals, 'yh', [(f, f - step) for f in range(step, FAR)])  3.88 us
    pallas_call x1, Pallas kernels, front(): pl.pallas_call(front_kernel, name='front', out_shape=(jax.ShapeDtypeStruc...  3.51 us
  transfers between devices with their start and end apart: 12, of which 5 were waited for; matrix products, arithmetic and copies ran while one was open for 0% of the time, Pallas kernels for 0%

profile of v6, /device:TPU:1, one launch (start us, length us, event | category | flops | bytes accessed | tf_op | source)
XLA Modules:
  0.0 65.9 jit_solution(15549532799154073741)
XLA Ops:
  0.6 3.5 %front.1 = (bf16[32,136,128]{2,1,0:T(8,128)(2,1)}, f32[1,128]{1,0:T(1,128)S(1)}) custom-call(s32[1,32]{1,0:T(1,128)} %order_hbm.1, f32[1,4]{1,0:T(1,128)} %head_gate_hbm.1, bf16[1,128,512]{2,1,0:T(8,128)(2,1)} %q_hbm.1, bf16[1,128,128]{2,1,0:T(8,128)(2,1)} %k_hbm.1, bf16[1,128,128]{2,1,0:T(8,128)(2,1)} %v_hbm.1, bf16[1,128,512]{2,1,0:T(8,128)(2,1)} %grad_hbm.1, ...), custom_call_target="tpu_custom_call" | custom-call | tf_op jit(solution)/shard_map/front/pallas_call | solution.py:119
  4.2 10.5 %all-to-all-start = ((bf16[32,136,128]{2,1,0:T(8,128)(2,1)}), bf16[32,136,128]{2,1,0:T(8,128)(2,1)S(1)}, u32[]{:S(2)}, u32[]{:S(2)}) async-start(bf16[32,136,128]{2,1,0:T(8,128)(2,1)} %get-tuple-element.17), calls=%async_computation | async-start | bytes 2228224 | tf_op jit(solution)/shard_map/all_to_all | solution.py:235
  15.3 2.2 %collective-permute-start = (f32[8,128]{1,0:T(8,128)S(1)}, f32[8,128]{1,0:T(8,128)S(1)}, u32[]{:S(2)}, u32[]{:S(2)}) collective-permute-start(f32[8,128]{1,0:T(8,128)S(1)} %broadcast_in_dim.9.own_ref.gate_ref), channel_id=1, source_target_pairs={{0,8},{8,0},{1,9},{9,1},{2,10},{10,2},{3,11},{11,3},{4,12},{12,4},... | collective-permute-start | bytes 12296 | tf_op jit(solution)/shard_map/ppermute | solution.py:238
  17.6 0.8 %collective-permute-done.core_ref = f32[8,128]{1,0:T(8,128)S(1)} collective-permute-done((f32[8,128]{1,0:T(8,128)S(1)}, f32[8,128]{1,0:T(8,128)S(1)}, u32[]{:S(2)}, u32[]{:S(2)}) %collective-permute-start) | collective-permute-done | bytes 4128 | tf_op jit(solution)/shard_map/ppermute | solution.py:238
  18.4 3.3 %collective-permute-start.1 = (f32[8,128]{1,0:T(8,128)S(1)}, f32[8,128]{1,0:T(8,128)S(1)}, u32[]{:S(2)}, u32[]{:S(2)}) collective-permute-start(f32[8,128]{1,0:T(8,128)S(1)} %gate_pair.1.gates_ref), channel_id=1, source_target_pairs={{0,64},{64,0},{1,65},{65,1},{2,66},{66,2},{3,67},{67,3},{4,68},{68... | collective-permute-start | bytes 12296 | tf_op jit(solution)/shard_map/ppermute | solution.py:242
  21.7 7.2 %collective-permute-done.1.y_gates_ref = f32[8,128]{1,0:T(8,128)S(1)} collective-permute-done((f32[8,128]{1,0:T(8,128)S(1)}, f32[8,128]{1,0:T(8,128)S(1)}, u32[]{:S(2)}, u32[]{:S(2)}) %collective-permute-start.1) | collective-permute-done | bytes 4128 | tf_op jit(solution)/shard_map/ppermute | solution.py:242
  28.9 2.8 %all-to-all-done.parts_ref = bf16[32,136,128]{2,1,0:T(8,128)(2,1)S(1)} async-done(((bf16[32,136,128]{2,1,0:T(8,128)(2,1)}), bf16[32,136,128]{2,1,0:T(8,128)(2,1)S(1)}, u32[]{:S(2)}, u32[]{:S(2)}) %all-to-all-start) | async-done | bytes 1114144 | tf_op jit(solution)/shard_map/all_to_all | solution.py:235
  31.7 0.2 terms.1
  31.9 1.3 %collective-permute-start.2 = (bf16[128,128]{1,0:T(8,128)(2,1)S(1)}, bf16[128,128]{1,0:T(8,128)(2,1)S(1)}, u32[]{:S(2)}, u32[]{:S(2)}) collective-permute-start(bf16[128,128]{1,0:T(8,128)(2,1)S(1)} %get-tuple-element.20), channel_id=1, source_target_pairs={{384,0},{385,1},{386,2},{387,3},{388,4},{389,5},{390,6},{391,7},{3... | collective-permute-start | bytes 98312 | tf_op jit(solution)/shard_map/ppermute | solution.py:255
  33.2 1.3 %collective-permute-start.3 = (bf16[128,128]{1,0:T(8,128)(2,1)S(1)}, bf16[128,128]{1,0:T(8,128)(2,1)S(1)}, u32[]{:S(2)}, u32[]{:S(2)}) collective-permute-start(bf16[128,128]{1,0:T(8,128)(2,1)S(1)} %get-tuple-element.20), channel_id=1, source_target_pairs={{256,0},{384,128},{257,1},{385,129},{258,2},{386,130},{259,3},{387... | collective-permute-start | bytes 98312 | tf_op jit(solution)/shard_map/ppermute | solution.py:255
  34.5 1.3 %collective-permute-start.4 = (bf16[128,128]{1,0:T(8,128)(2,1)S(1)}, bf16[128,128]{1,0:T(8,128)(2,1)S(1)}, u32[]{:S(2)}, u32[]{:S(2)}) collective-permute-start(bf16[128,128]{1,0:T(8,128)(2,1)S(1)} %get-tuple-element.20), channel_id=1, source_target_pairs={{128,0},{256,128},{384,256},{129,1},{257,129},{385,257},{130,2},{2... | collective-permute-start | bytes 98312 | tf_op jit(solution)/shard_map/ppermute | solution.py:255
  35.8 2.9 %collective-permute-done.2.far_1 = bf16[128,128]{1,0:T(8,128)(2,1)S(1)} collective-permute-done((bf16[128,128]{1,0:T(8,128)(2,1)S(1)}, bf16[128,128]{1,0:T(8,128)(2,1)S(1)}, u32[]{:S(2)}, u32[]{:S(2)}) %collective-permute-start.2) | collective-permute-done | bytes 32800 | tf_op jit(solution)/shard_map/ppermute | solution.py:255
  38.7 3.2 %collective-permute-done.3.far_2 = bf16[128,128]{1,0:T(8,128)(2,1)S(1)} collective-permute-done((bf16[128,128]{1,0:T(8,128)(2,1)S(1)}, bf16[128,128]{1,0:T(8,128)(2,1)S(1)}, u32[]{:S(2)}, u32[]{:S(2)}) %collective-permute-start.3) | collective-permute-done | bytes 32800 | tf_op jit(solution)/shard_map/ppermute | solution.py:255
  41.9 0.0 collective-permute-done.4.far_3
  41.9 1.3 %collective-permute-start.5 = (bf16[2,128,128]{2,1,0:T(8,128)(2,1)S(1)}, bf16[2,128,128]{2,1,0:T(8,128)(2,1)S(1)}, u32[]{:S(2)}, u32[]{:S(2)}) collective-permute-start(bf16[2,128,128]{2,1,0:T(8,128)(2,1)S(1)} %get-tuple-element.22), channel_id=1, source_target_pairs={{48,0},{32,16},{49,1},{33,17},{50,2},{34,18},{51,3},{35,19},{52,4}... | collective-permute-start | bytes 196616 | tf_op jit(solution)/shard_map/ppermute | solution.py:269
  43.2 1.3 %collective-permute-start.6 = (bf16[2,128,128]{2,1,0:T(8,128)(2,1)S(1)}, bf16[2,128,128]{2,1,0:T(8,128)(2,1)S(1)}, u32[]{:S(2)}, u32[]{:S(2)}) collective-permute-start(bf16[2,128,128]{2,1,0:T(8,128)(2,1)S(1)} %get-tuple-element.22), channel_id=1, source_target_pairs={{32,0},{48,16},{33,1},{49,17},{34,2},{50,18},{35,3},{51,19},{36,4}... | collective-permute-start | bytes 196616 | tf_op jit(solution)/shard_map/ppermute | solution.py:270
  44.5 3.9 %collective-permute-start.7 = (bf16[2,128,128]{2,1,0:T(8,128)(2,1)S(1)}, bf16[2,128,128]{2,1,0:T(8,128)(2,1)S(1)}, u32[]{:S(2)}, u32[]{:S(2)}) collective-permute-start(bf16[2,128,128]{2,1,0:T(8,128)(2,1)S(1)} %get-tuple-element.23), channel_id=1, source_target_pairs={{0,16},{16,0},{1,17},{17,1},{2,18},{18,2},{3,19},{19,3},{4,20},{20... | collective-permute-start | bytes 196616 | tf_op jit(solution)/shard_map/ppermute | solution.py:271
  48.4 4.6 %collective-permute-start.9 = (bf16[2,128,128]{2,1,0:T(8,128)(2,1)S(1)}, bf16[2,128,128]{2,1,0:T(8,128)(2,1)S(1)}, u32[]{:S(2)}, u32[]{:S(2)}) collective-permute-start(bf16[2,128,128]{2,1,0:T(8,128)(2,1)S(1)} %get-tuple-element.23), channel_id=1, source_target_pairs={{0,48},{1,49},{2,50},{3,51},{4,52},{5,53},{6,54},{7,55},{8,56},{9,... | collective-permute-start | bytes 196616 | tf_op jit(solution)/shard_map/ppermute | solution.py:279
  53.0 0.7 %collective-permute-start.8 = (bf16[2,128,128]{2,1,0:T(8,128)(2,1)S(1)}, bf16[2,128,128]{2,1,0:T(8,128)(2,1)S(1)}, u32[]{:S(2)}, u32[]{:S(2)}) collective-permute-start(bf16[2,128,128]{2,1,0:T(8,128)(2,1)S(1)} %get-tuple-element.25), channel_id=1, source_target_pairs={{48,32},{16,48},{49,33},{17,49},{50,34},{18,50},{51,35},{19,51},{5... | collective-permute-start | bytes 196616 | tf_op jit(solution)/shard_map/ppermute | solution.py:278
  53.7 0.0 collective-permute-done.5.step_1
  53.7 0.0 collective-permute-done.6.step_2
  53.7 0.0 collective-permute-done.7.step_3
  53.8 0.1 pass_on.1
  53.8 0.7 %collective-permute-start.10 = (bf16[2,128,128]{2,1,0:T(8,128)(2,1)S(1)}, bf16[2,128,128]{2,1,0:T(8,128)(2,1)S(1)}, u32[]{:S(2)}, u32[]{:S(2)}) collective-permute-start(bf16[2,128,128]{2,1,0:T(8,128)(2,1)S(1)} %get-tuple-element.26), channel_id=1, source_target_pairs={{16,32},{32,48},{17,33},{33,49},{18,34},{34,50},{19,35},{35,51},{2... | collective-permute-start | bytes 196616 | tf_op jit(solution)/shard_map/ppermute | solution.py:280
  54.5 0.0 collective-permute-done.8.step_5
  54.5 0.0 collective-permute-done.9.step_6
  54.5 0.0 collective-permute-done.10.step_4
  54.5 0.1 sums.1
  54.6 10.6 %all_to_all.10.blocks_ref = bf16[4,128,128]{2,1,0:T(8,128)(2,1)S(1)} all-to-all(bf16[4,128,128]{2,1,0:T(8,128)(2,1)S(1)} %sums.1), channel_id=1, replica_groups=mesh['yh'=4,'yl'=2,'zh'=4,'core'=2,'zl'=2,'x'=4] {'core','yl'}, dimensions={0} | all-to-all | bytes 262144 | tf_op jit(solution)/shard_map/all_to_all | solution.py:284
  65.2 0.7 %join.1 = (bf16[1,128,512]{2,1,0:T(8,128)(2,1)}, f32[1,4]{1,0:T(1,128)}, f32[1]{0:T(128)}) custom-call(bf16[4,128,128]{2,1,0:T(8,128)(2,1)S(1)} %all_to_all.10.blocks_ref, f32[8,128]{1,0:T(8,128)S(1)} %get-tuple-element.27.share_ref, f32[8,128]{1,0:T(8,128)S(1)} %broadcast_in_dim.9.own_ref.gate_ref, f32[1,128]{1,0:T(1,128)S(1)} %get-tuple-element.28.head_sum_ref), custom_call_target="tpu_custom_call" | custom-call | tf_op jit(solution)/shard_map/join/pallas_call | solution.py:285
  (3 shorter events, 0.1 us)
Async XLA Ops:
  4.2 27.6 %all-to-all-start = ((bf16[32,136,128]{2,1,0:T(8,128)(2,1)}), bf16[32,136,128]{2,1,0:T(8,128)(2,1)S(1)}, u32[]{:S(2)}, u32[]{:S(2)}) async-start(bf16[32,136,128]{2,1,0:T(8,128)(2,1)} %get-tuple-element.17), calls=%async_computation | async-start | bytes 2228224 | tf_op jit(solution)/shard_map/all_to_all | solution.py:235
  15.3 3.1 %collective-permute-start = (f32[8,128]{1,0:T(8,128)S(1)}, f32[8,128]{1,0:T(8,128)S(1)}, u32[]{:S(2)}, u32[]{:S(2)}) collective-permute-start(f32[8,128]{1,0:T(8,128)S(1)} %broadcast_in_dim.9.own_ref.gate_ref), channel_id=1, source_target_pairs={{0,8},{8,0},{1,9},{9,1},{2,10},{10,2},{3,11},{11,3},{4,12},{12,4},... | collective-permute-start | bytes 12296 | tf_op jit(solution)/shard_map/ppermute | solution.py:238
  18.4 10.5 %collective-permute-start.1 = (f32[8,128]{1,0:T(8,128)S(1)}, f32[8,128]{1,0:T(8,128)S(1)}, u32[]{:S(2)}, u32[]{:S(2)}) collective-permute-start(f32[8,128]{1,0:T(8,128)S(1)} %gate_pair.1.gates_ref), channel_id=1, source_target_pairs={{0,64},{64,0},{1,65},{65,1},{2,66},{66,2},{3,67},{67,3},{4,68},{68... | collective-permute-start | bytes 12296 | tf_op jit(solution)/shard_map/ppermute | solution.py:242
  31.9 6.8 %collective-permute-start.2 = (bf16[128,128]{1,0:T(8,128)(2,1)S(1)}, bf16[128,128]{1,0:T(8,128)(2,1)S(1)}, u32[]{:S(2)}, u32[]{:S(2)}) collective-permute-start(bf16[128,128]{1,0:T(8,128)(2,1)S(1)} %get-tuple-element.20), channel_id=1, source_target_pairs={{384,0},{385,1},{386,2},{387,3},{388,4},{389,5},{390,6},{391,7},{3... | collective-permute-start | bytes 98312 | tf_op jit(solution)/shard_map/ppermute | solution.py:255
  33.2 8.7 %collective-permute-start.3 = (bf16[128,128]{1,0:T(8,128)(2,1)S(1)}, bf16[128,128]{1,0:T(8,128)(2,1)S(1)}, u32[]{:S(2)}, u32[]{:S(2)}) collective-permute-start(bf16[128,128]{1,0:T(8,128)(2,1)S(1)} %get-tuple-element.20), channel_id=1, source_target_pairs={{256,0},{384,128},{257,1},{385,129},{258,2},{386,130},{259,3},{387... | collective-permute-start | bytes 98312 | tf_op jit(solution)/shard_map/ppermute | solution.py:255
  34.5 7.4 %collective-permute-start.4 = (bf16[128,128]{1,0:T(8,128)(2,1)S(1)}, bf16[128,128]{1,0:T(8,128)(2,1)S(1)}, u32[]{:S(2)}, u32[]{:S(2)}) collective-permute-start(bf16[128,128]{1,0:T(8,128)(2,1)S(1)} %get-tuple-element.20), channel_id=1, source_target_pairs={{128,0},{256,128},{384,256},{129,1},{257,129},{385,257},{130,2},{2... | collective-permute-start | bytes 98312 | tf_op jit(solution)/shard_map/ppermute | solution.py:255
  41.9 11.8 %collective-permute-start.5 = (bf16[2,128,128]{2,1,0:T(8,128)(2,1)S(1)}, bf16[2,128,128]{2,1,0:T(8,128)(2,1)S(1)}, u32[]{:S(2)}, u32[]{:S(2)}) collective-permute-start(bf16[2,128,128]{2,1,0:T(8,128)(2,1)S(1)} %get-tuple-element.22), channel_id=1, source_target_pairs={{48,0},{32,16},{49,1},{33,17},{50,2},{34,18},{51,3},{35,19},{52,4}... | collective-permute-start | bytes 196616 | tf_op jit(solution)/shard_map/ppermute | solution.py:269
  43.2 10.5 %collective-permute-start.6 = (bf16[2,128,128]{2,1,0:T(8,128)(2,1)S(1)}, bf16[2,128,128]{2,1,0:T(8,128)(2,1)S(1)}, u32[]{:S(2)}, u32[]{:S(2)}) collective-permute-start(bf16[2,128,128]{2,1,0:T(8,128)(2,1)S(1)} %get-tuple-element.22), channel_id=1, source_target_pairs={{32,0},{48,16},{33,1},{49,17},{34,2},{50,18},{35,3},{51,19},{36,4}... | collective-permute-start | bytes 196616 | tf_op jit(solution)/shard_map/ppermute | solution.py:270
  44.5 9.2 %collective-permute-start.7 = (bf16[2,128,128]{2,1,0:T(8,128)(2,1)S(1)}, bf16[2,128,128]{2,1,0:T(8,128)(2,1)S(1)}, u32[]{:S(2)}, u32[]{:S(2)}) collective-permute-start(bf16[2,128,128]{2,1,0:T(8,128)(2,1)S(1)} %get-tuple-element.23), channel_id=1, source_target_pairs={{0,16},{16,0},{1,17},{17,1},{2,18},{18,2},{3,19},{19,3},{4,20},{20... | collective-permute-start | bytes 196616 | tf_op jit(solution)/shard_map/ppermute | solution.py:271
  48.4 6.1 %collective-permute-start.9 = (bf16[2,128,128]{2,1,0:T(8,128)(2,1)S(1)}, bf16[2,128,128]{2,1,0:T(8,128)(2,1)S(1)}, u32[]{:S(2)}, u32[]{:S(2)}) collective-permute-start(bf16[2,128,128]{2,1,0:T(8,128)(2,1)S(1)} %get-tuple-element.23), channel_id=1, source_target_pairs={{0,48},{1,49},{2,50},{3,51},{4,52},{5,53},{6,54},{7,55},{8,56},{9,... | collective-permute-start | bytes 196616 | tf_op jit(solution)/shard_map/ppermute | solution.py:279
  53.0 1.4 %collective-permute-start.8 = (bf16[2,128,128]{2,1,0:T(8,128)(2,1)S(1)}, bf16[2,128,128]{2,1,0:T(8,128)(2,1)S(1)}, u32[]{:S(2)}, u32[]{:S(2)}) collective-permute-start(bf16[2,128,128]{2,1,0:T(8,128)(2,1)S(1)} %get-tuple-element.25), channel_id=1, source_target_pairs={{48,32},{16,48},{49,33},{17,49},{50,34},{18,50},{51,35},{19,51},{5... | collective-permute-start | bytes 196616 | tf_op jit(solution)/shard_map/ppermute | solution.py:278
  53.8 0.7 %collective-permute-start.10 = (bf16[2,128,128]{2,1,0:T(8,128)(2,1)S(1)}, bf16[2,128,128]{2,1,0:T(8,128)(2,1)S(1)}, u32[]{:S(2)}, u32[]{:S(2)}) collective-permute-start(bf16[2,128,128]{2,1,0:T(8,128)(2,1)S(1)} %get-tuple-element.26), channel_id=1, source_target_pairs={{16,32},{32,48},{17,33},{33,49},{18,34},{34,50},{19,35},{35,51},{2... | collective-permute-start | bytes 196616 | tf_op jit(solution)/shard_map/ppermute | solution.py:280
